TPU v7x, 512 devices: a whole 4x8x8 slice. The times are simulated.
512 devices in a mesh: gz: 16 (over z_hi, x), ta: 32 (over y, z_lo, core).
Axes of the slice: x: 4, y: 8, z: 8 (z_hi: 4, z_lo: 2; z = z_hi * 2 + z_lo), core: 2. Of those that a mesh axis runs over, the one named last changes fastest.
Arguments:
- low_modes: bfloat16 [16, 2, 4, 3, 64, 32, 256], P(None, None, None, None, 'ta', 'gz'), may hold values from -6 to 6
- gauge_links: float32 [4, 18, 64, 32, 256], P(None, None, 'ta', 'gz'), may hold values from -2.5 to 2.5
- photon: float32 [4, 64, 32, 256], P(None, 'ta', 'gz'), may hold values from -5 to 5
- charges: int32 [16], replicated, may hold values from -2 to 2, as said below
- window_start: int32 [1], replicated, may hold values from 0 to 63
Outputs:
- insert_one: float32 [2, 16, 16], replicated
- insert_two: float32 [2, 16, 16], replicated
- window_one: float32 [2, 16, 16], replicated
- window_two: float32 [2, 16, 16], replicated
Inputs may be any that keep to these rules, and one draw needn't show every extreme that they name: `charges`: never 0.
All inputs are finite; a program needn't handle non-finite values.
Results may differ from a plain program's by a relative error of at most 0.0003.
Values may be sent and summed in bfloat16 or wider, within the bound.
A program may use at most 64 MiB of HBM per device.

v0:
```python
import math

import jax
import jax.numpy as jnp
import numpy as np
from jax import lax
from jax.sharding import PartitionSpec as P

LY = 16
TW = 4


def shifted(shard, axis, by):
    peers = lax.axis_size(axis)
    return lax.ppermute(shard, axis, [(i, (i + by) % peers) for i in range(peers)])


def with_halo(block, sides, width):
    for axis, dim in sides:
        count = lax.axis_size(axis)
        forward = [(i, i + 1) for i in range(count - 1)]
        forward.append((count - 1, 0))
        backward = [(target, source) for source, target in forward]
        low = lax.ppermute(
            lax.slice_in_dim(block, block.shape[dim] - width, None, axis=dim), axis, forward
        )
        high = lax.ppermute(lax.slice_in_dim(block, 0, width, axis=dim), axis, backward)
        block = jnp.concatenate([low, block, high], axis=dim)
    return block


def gamma_tables():
    table_real = np.zeros((4, 4, 4))
    table_imag = np.zeros((4, 4, 4))
    table_imag[0, 0, 3] = 1.0
    table_imag[0, 1, 2] = 1.0
    table_imag[0, 2, 1] = -1.0
    table_imag[0, 3, 0] = -1.0
    table_real[1, 0, 3] = -1.0
    table_real[1, 1, 2] = 1.0
    table_real[1, 2, 1] = 1.0
    table_real[1, 3, 0] = -1.0
    table_imag[2, 0, 2] = 1.0
    table_imag[2, 1, 3] = -1.0
    table_imag[2, 2, 0] = -1.0
    table_imag[2, 3, 1] = 1.0
    table_real[3, 0, 2] = 1.0
    table_real[3, 1, 3] = 1.0
    table_real[3, 2, 0] = 1.0
    table_real[3, 3, 1] = 1.0
    return (table_real, table_imag)


def color_apply(link_data, values, adjoint):
    rows_real = []
    rows_imag = []
    for a in range(3):
        sum_real = 0.0
        sum_imag = 0.0
        for b in range(3):
            if adjoint:
                link_real = link_data[b * 3 + a]
                link_imag = -link_data[9 + b * 3 + a]
            else:
                link_real = link_data[a * 3 + b]
                link_imag = link_data[9 + a * 3 + b]
            part_real = values[:, 0, :, b]
            part_imag = values[:, 1, :, b]
            sum_real = sum_real + link_real * part_real - link_imag * part_imag
            sum_imag = sum_imag + link_real * part_imag + link_imag * part_real
        rows_real.append(sum_real)
        rows_imag.append(sum_imag)
    return jnp.stack([jnp.stack(rows_real, axis=2), jnp.stack(rows_imag, axis=2)], axis=1)


def spin_apply(direction, sign_factor, values):
    table_real, table_imag = gamma_tables()
    spins_real = []
    spins_imag = []
    for s in range(4):
        spin_real = values[:, 0, s]
        spin_imag = values[:, 1, s]
        for k in range(4):
            entry_real = sign_factor * float(table_real[direction, s, k])
            entry_imag = sign_factor * float(table_imag[direction, s, k])
            if entry_real != 0.0:
                spin_real = spin_real + entry_real * values[:, 0, k]
                spin_imag = spin_imag + entry_real * values[:, 1, k]
            if entry_imag != 0.0:
                spin_real = spin_real - entry_imag * values[:, 1, k]
                spin_imag = spin_imag + entry_imag * values[:, 0, k]
        spins_real.append(spin_real)
        spins_imag.append(spin_imag)
    return jnp.stack([jnp.stack(spins_real, axis=1), jnp.stack(spins_imag, axis=1)], axis=1)


def shift_xy(values, direction, in_front, last_y, first_y):
    if direction == 0:
        return jnp.roll(values, -LY if in_front else LY, axis=-1)
    if in_front:
        return jnp.where(last_y, jnp.roll(values, LY - 1, axis=-1), jnp.roll(values, -1, axis=-1))
    return jnp.where(first_y, jnp.roll(values, 1 - LY, axis=-1), jnp.roll(values, 1, axis=-1))


def minus_i(values):
    return jnp.stack([values[:, 1], -values[:, 0]], axis=1)


def plane_hops(centre, link_data, first_order, second_order):
    sites_xy = centre.shape[-1]
    column = jnp.arange(sites_xy) % LY
    last_y = column == LY - 1
    first_y = column == 0
    for direction in range(2):
        in_front = shift_xy(centre, direction, True, last_y, first_y)
        behind = shift_xy(centre, direction, False, last_y, first_y)
        link_here = link_data[direction]
        link_behind = shift_xy(link_here, direction, False, last_y, first_y)
        forward = spin_apply(direction, -1.0, color_apply(link_here, in_front, False))
        backward = spin_apply(direction, 1.0, color_apply(link_behind, behind, True))
        photon_here = link_here[18]
        photon_behind = link_behind[18]
        difference = photon_here * forward - photon_behind * backward
        first_order = first_order + 0.5 * minus_i(difference)
        second_order = second_order + 0.25 * (
            photon_here * photon_here * forward + photon_behind * photon_behind * backward
        )
    return (first_order, second_order)


def insert_block(padded, padded_links, charge):
    values = padded.astype(jnp.float32)
    centre = values[:, :, :, :, 1:-1, 1:-1, :]
    link_mid = padded_links[:, :, 1:-1, 1:-1, :]
    first_order, second_order = plane_hops(
        centre, link_mid, jnp.zeros_like(centre), jnp.zeros_like(centre)
    )
    for direction in (2, 3):
        if direction == 2:
            in_front = values[:, :, :, :, 1:-1, 2:, :]
            behind = values[:, :, :, :, 1:-1, :-2, :]
            link_behind = padded_links[direction, :, 1:-1, :-2, :]
        else:
            in_front = values[:, :, :, :, 2:, 1:-1, :]
            behind = values[:, :, :, :, :-2, 1:-1, :]
            link_behind = padded_links[direction, :, :-2, 1:-1, :]
        link_here = link_mid[direction]
        forward = spin_apply(direction, -1.0, color_apply(link_here, in_front, False))
        backward = spin_apply(direction, 1.0, color_apply(link_behind, behind, True))
        photon_here = link_here[18]
        photon_behind = link_behind[18]
        difference = photon_here * forward - photon_behind * backward
        first_order = first_order + 0.5 * minus_i(difference)
        second_order = second_order + 0.25 * (
            photon_here * photon_here * forward + photon_behind * photon_behind * backward
        )
    charge_column = charge.reshape((-1, 1, 1, 1, 1, 1, 1))
    return (first_order * charge_column, second_order * charge_column * charge_column)


def contract_time(bra, ket, time_mask):
    products = lax.dot_general(
        bra,
        ket,
        (((2, 3, 5, 6), (2, 3, 5, 6)), ((4,), (4,))),
        precision=lax.Precision.HIGHEST,
        preferred_element_type=jnp.float32,
    )
    real_part = products[:, :, 0, :, 0] + products[:, :, 1, :, 1]
    imag_part = products[:, :, 0, :, 1] - products[:, :, 1, :, 0]
    per_time = jnp.stack([real_part, imag_part], axis=1)
    return (jnp.sum(per_time, axis=0), jnp.sum(per_time * time_mask[:, None, None, None], axis=0))


def antiperiodic(padded, position, rank_count):
    inner_rows = padded.shape[4] - 2
    low_sign = jnp.where(position == 0, -1.0, 1.0).astype(jnp.float32)
    high_sign = jnp.where(position == rank_count - 1, -1.0, 1.0).astype(jnp.float32)
    sign_rows = jnp.concatenate(
        [low_sign[None], jnp.ones((inner_rows,), jnp.float32), high_sign[None]]
    ).astype(jnp.bfloat16)
    return padded * sign_rows[:, None, None]


def lower_padded_links(link_data):
    slabs_t = link_data.shape[2]
    slabs_z = link_data.shape[3]
    rim_z = shifted(link_data[2:3, :, :, slabs_z - 1 : slabs_z, :], "gz", 1)
    rim_t = shifted(link_data[3:4, :, slabs_t - 1 : slabs_t, :, :], "ta", 1)
    rim_z_full = jnp.concatenate(
        [jnp.zeros((2,) + rim_z.shape[1:], jnp.float32), rim_z, jnp.zeros_like(rim_z)], axis=0
    )
    with_z = jnp.concatenate([rim_z_full, link_data, jnp.zeros_like(rim_z_full)], axis=3)
    rim_t_full = jnp.concatenate([jnp.zeros((3,) + rim_t.shape[1:], jnp.float32), rim_t], axis=0)
    edge_zero = jnp.zeros(rim_t_full.shape[:3] + (1,) + rim_t_full.shape[4:], jnp.float32)
    rim_t_wide = jnp.concatenate([edge_zero, rim_t_full, edge_zero], axis=3)
    return jnp.concatenate([rim_t_wide, with_z, jnp.zeros_like(rim_t_wide)], axis=2)


def per_device(low_modes, gauge_links, photon, charges, window_start):
    mode_count = low_modes.shape[0]
    slabs_t = low_modes.shape[4]
    slabs_z = low_modes.shape[5]
    sites_xy = low_modes.shape[6]
    rank_count = lax.axis_size("ta")
    lattice_t = slabs_t * rank_count
    lattice_z = slabs_z * lax.axis_size("gz")
    position = lax.axis_index("ta")
    start = window_start[0]
    groups = mode_count // 8
    charge = charges.astype(jnp.float32) / 3.0
    charge_groups = charge.reshape(groups, 8)
    t_global = position * slabs_t + jnp.arange(slabs_t, dtype=jnp.int32)
    time_mask = ((t_global - start) % lattice_t < TW).astype(jnp.float32)
    link_data = jnp.concatenate([gauge_links, photon[:, None]], axis=1)
    bra = low_modes.astype(jnp.float32)
    padded_links = lower_padded_links(link_data)
    padded = antiperiodic(with_halo(low_modes, (("gz", 5), ("ta", 4)), 1), position, rank_count)
    stacked = padded.reshape((groups, 8) + padded.shape[1:])

    def one_group(group_pair):
        first_order, second_order = insert_block(group_pair[0], padded_links, group_pair[1])
        one_all, one_window = contract_time(bra, first_order, time_mask)
        two_all, two_window = contract_time(bra, second_order, time_mask)
        return jnp.stack([one_all, two_all, one_window, two_window])

    results = lax.map(one_group, (stacked, charge_groups))
    matrices = jnp.transpose(results, (1, 2, 3, 0, 4)).reshape(4, 2, mode_count, mode_count)
    one_all = matrices[0]
    two_all = matrices[1]
    one_window = matrices[2]
    two_window = matrices[3]
    one_total, two_total, one_wsum, two_wsum = lax.psum(
        (one_all, two_all, one_window, two_window), ("gz", "ta")
    )
    main_scale = 1.0 / math.sqrt(24.0 * lattice_t * lattice_z * sites_xy)
    window_scale = 1.0 / math.sqrt(24.0 * TW * lattice_z * sites_xy)
    return (
        one_total * main_scale,
        two_total * main_scale,
        one_wsum * window_scale,
        two_wsum * window_scale,
    )


def solution(mesh):
    return jax.shard_map(
        per_device,
        mesh=mesh,
        in_specs=(
            P(None, None, None, None, "ta", "gz", None),
            P(None, None, "ta", "gz", None),
            P(None, "ta", "gz", None),
            P(),
            P(),
        ),
        out_specs=(P(), P(), P(), P()),
        check_vma=False,
    )
```

profile of v0, /device:TPU:1, one launch (start us, length us, event | category | flops | bytes accessed | tf_op | source)
XLA Modules:
  0.0 214.1 jit_solution(13304609683046013982)
XLA Ops:
  0.7 3.0 %fusion.143 = (bf16[16,2,4,3,2,1,256]{6,5,4,3,2,1,0:T(2,128)(2,1)S(1)}, bf16[16,2,4,3,2,1,256]{6,5,4,3,2,1,0:T(2,128)(2,1)S(1)}) fusion(bf16[16,2,4,3,2,2,256]{6,5,4,3,2,1,0:T(2,128)(2,1)} %param.7), kind=kLoop, calls=%fused_computation.600 | loop fusion | bytes 1572864 | tf_op jit(solution)/shard_map/slice | solution.py:27
  3.7 0.4 copy.101
  4.1 4.1 %collective-permute-start = (bf16[16,2,4,3,2,1,256]{6,0,5,3,2,1,4:T(8,128)(2,1)S(1)}, bf16[16,2,4,3,2,1,256]{6,0,5,3,2,1,4:T(8,128)(2,1)S(1)}, u32[]{:S(2)}, u32[]{:S(2)}) collective-permute-start(bf16[16,2,4,3,2,1,256]{6,0,5,3,2,1,4:T(8,128)(2,1)S(1)} %copy.101), channel_id=1, source_target_pairs={{0,32},{32,64},{64,96},{96,128},{128,160},{160,192},{192,224},{224... | collective-permute-start | bytes 1179656 | tf_op jit(solution)/shard_map/ppermute | solution.py:24
  8.2 1.2 copy.102
  9.4 11.6 %collective-permute-start.1 = (bf16[16,2,4,3,2,1,256]{6,0,5,3,2,1,4:T(8,128)(2,1)}, bf16[16,2,4,3,2,1,256]{6,0,5,3,2,1,4:T(8,128)(2,1)}, u32[]{:S(2)}, u32[]{:S(2)}) collective-permute-start(bf16[16,2,4,3,2,1,256]{6,0,5,3,2,1,4:T(8,128)(2,1)} %copy.102), channel_id=1, source_target_pairs={{32,0},{64,32},{96,64},{128,96},{160,128},{192,160},{224,192},{256... | collective-permute-start | bytes 1179656 | tf_op jit(solution)/shard_map/ppermute | solution.py:27
  21.1 1.9 collective-permute-start.4
  23.1 3.9 %collective-permute-start.5 = (f32[1,19,1,2,256]{4,3,2,1,0:T(2,128)S(1)}, f32[1,19,1,2,256]{4,3,2,1,0:T(2,128)S(1)}, u32[]{:S(2)}, u32[]{:S(2)}) collective-permute-start(f32[1,19,1,2,256]{4,3,2,1,0:T(2,128)S(1)} %fusion.102), channel_id=1, source_target_pairs={{0,1},{1,2},{2,3},{3,4},{4,5},{5,6},{6,7},{7,8},{8,9},{9,10},{10,1... | collective-permute-start | bytes 116744 | tf_op jit(solution)/shard_map/ppermute | solution.py:15
  27.8 0.2 pad_maximum_fusion.14
  28.4 2.5 %collective-permute-done.4 = f32[1,19,2,1,256]{4,3,2,1,0:T(1,128)S(1)} collective-permute-done((f32[1,19,2,1,256]{4,3,2,1,0:T(1,128)S(1)}, f32[1,19,2,1,256]{4,3,2,1,0:T(1,128)S(1)}, u32[]{:S(2)}, u32[]{:S(2)}) %collective-permute-start.4) | collective-permute-done | bytes 38944 | tf_op jit(solution)/shard_map/ppermute | solution.py:15
  31.1 0.9 copy_convert_fusion
  32.0 1.5 collective-permute-done.1
  33.6 1.0 constant_dynamic-update-slice_fusion
  34.7 8.6 %collective-permute-start.3 = (bf16[16,2,4,3,1,4,256]{6,0,5,3,2,1,4:T(8,128)(2,1)S(1)}, bf16[16,2,4,3,1,4,256]{6,0,5,3,2,1,4:T(8,128)(2,1)S(1)}, u32[]{:S(2)}, u32[]{:S(2)}) collective-permute-start(bf16[16,2,4,3,1,4,256]{6,0,5,3,2,1,4:T(8,128)(2,1)S(1)} %get-tuple-element.835), channel_id=1, source_target_pairs={{1,0},{2,1},{3,2},{4,3},{5,4},{6,5},{7,6},{8,7},{9,8},{10,9},{11,1... | collective-permute-start | bytes 2359304 | tf_op jit(solution)/shard_map/ppermute | solution.py:27
  43.3 1.9 collective-permute-start.2
  45.4 0.4 pad_maximum_fusion.12
  45.9 1.5 fusion.94
  47.4 0.9 fusion.114
  48.4 12.7 %collective-permute-done.3 = bf16[16,2,4,3,1,4,256]{6,0,5,3,2,1,4:T(8,128)(2,1)S(1)} collective-permute-done((bf16[16,2,4,3,1,4,256]{6,0,5,3,2,1,4:T(8,128)(2,1)S(1)}, bf16[16,2,4,3,1,4,256]{6,0,5,3,2,1,4:T(8,128)(2,1)S(1)}, u32[]{:S(2)}, u32[]{:S(2)}) %collective-permute-start.3) | collective-permute-done | bytes 786464 | tf_op jit(solution)/shard_map/ppermute | solution.py:27
  61.0 0.8 collective-permute-done.2
  61.9 1.8 maximum_multiply_fusion
  63.7 47.6 %while.13 = (s32[]{:T(128)}, f32[2,4,2,16,8]{3,4,0,2,1:T(8,128)S(1)}, f32[4,19,2,2,256]{4,3,2,1,0:T(2,128)S(1)}, bf16[2,8,2,4,3,4,4,256]{7,1,0,6,5,4,3,2:T(8,128...) while((s32[]{:T(128)}, ...), condition=%wide.region_5.6_spmd.clone, body=%wide.region_0.5_spmd.clone.sunk | while | flops 191536688 | bytes 112994248 | solution.py:227
  63.7 1.8 fusion.193
  65.5 0.3 fusion.194
  65.8 0.2 fusion.195
  66.0 0.3 multiply_add_fusion.61
  66.3 0.2 multiply_add_fusion.62
  66.8 0.2 multiply_add_fusion.63
  67.0 0.2 multiply_add_fusion.64
  67.6 0.2 multiply_subtract_fusion.53
  67.8 0.3 fusion.198
  68.1 0.2 fusion.199
  68.5 0.3 fusion.201
  68.8 0.7 maximum_select_fusion.3
  70.8 0.2 multiply_subtract_fusion.60
  72.4 0.2 multiply_subtract_fusion.62
  72.7 0.9 slice_bitcast_fusion.221
  74.8 0.2 multiply_subtract_fusion.66
  75.1 5.7 %fusion.216 = f32[2,8,2,16,2,1,1,1]{3,1,7,6,0,4,2,5:T(8,128)S(1)} fusion(f32[16,2,4,3,2,2,256]{6,0,5,3,2,1,4:T(8,128)S(1)} %get-tuple-element.1842, f32[8,1,4,3,2,2,256]{6,0,5,4,3,2,1:T(8,128)S(1)} %get-tuple-element.1511, f32[8,1,4,3,2,2,256]{6,0,5,4,3,2,1:T(8,128)S(1)} %get-tuple-element.1512, ...), kind=kOutput, calls=%fused_computation.5.clone.1 | convolution fusion | flops 77070336 | bytes 4722720 | tf_op jit(solution)/shard_map/while/body/eval_jaxpr/dot_general | solution.py:162
  80.8 0.7 compare_convert_fusion.2
  81.5 5.9 %fusion.220 = f32[2,8,2,16,2]{3,1,4,0,2:T(8,128)S(1)} fusion(f32[16,2,4,3,2,2,256]{6,0,5,3,2,1,4:T(8,128)S(1)} %get-tuple-element.1842, f32[8,1,4,3,2,2,256]{6,0,5,4,3,2,1:T(8,128)S(1)} %get-tuple-element.1661, f32[8,1,4,3,2,2,256]{6,0,5,4,3,2,1:T(8,128)S(1)} %get-tuple-element.1662, f32[8,1,4,3,2,2,256]{6,0,5,4,3,2,1:T(8,128)S(1)} %maximum_bitcast_fusion.83, ...), kind=kOutput, calls=%fused_computation.17.clone.1 | convolution fusion | flops 80412672 | bytes 7901248 | tf_op jit(solution)/shard_map/while/body/eval_jaxpr/dot_general | solution.py:162
  87.5 1.8 fusion.193
  89.3 0.3 fusion.194
  89.6 0.2 fusion.195
  89.8 0.3 multiply_add_fusion.61
  90.1 0.2 multiply_add_fusion.62
  90.7 0.2 multiply_add_fusion.63
  90.9 0.2 multiply_add_fusion.64
  91.4 0.2 multiply_subtract_fusion.53
  91.6 0.3 fusion.198
  91.9 0.2 fusion.199
  92.3 0.3 fusion.201
  92.6 0.7 maximum_select_fusion.3
  94.6 0.2 multiply_subtract_fusion.60
  96.2 0.2 multiply_subtract_fusion.62
  96.5 0.9 slice_bitcast_fusion.221
  98.6 0.2 multiply_subtract_fusion.66
  98.9 5.7 %fusion.216 = f32[2,8,2,16,2,1,1,1]{3,1,7,6,0,4,2,5:T(8,128)S(1)} fusion(f32[16,2,4,3,2,2,256]{6,0,5,3,2,1,4:T(8,128)S(1)} %get-tuple-element.1842, f32[8,1,4,3,2,2,256]{6,0,5,4,3,2,1:T(8,128)S(1)} %get-tuple-element.1511, f32[8,1,4,3,2,2,256]{6,0,5,4,3,2,1:T(8,128)S(1)} %get-tuple-element.1512, ...), kind=kOutput, calls=%fused_computation.5.clone.1 | convolution fusion | flops 77070336 | bytes 4722720 | tf_op jit(solution)/shard_map/while/body/eval_jaxpr/dot_general | solution.py:162
  104.7 0.7 compare_convert_fusion.2
  105.4 5.9 %fusion.220 = f32[2,8,2,16,2]{3,1,4,0,2:T(8,128)S(1)} fusion(f32[16,2,4,3,2,2,256]{6,0,5,3,2,1,4:T(8,128)S(1)} %get-tuple-element.1842, f32[8,1,4,3,2,2,256]{6,0,5,4,3,2,1:T(8,128)S(1)} %get-tuple-element.1661, f32[8,1,4,3,2,2,256]{6,0,5,4,3,2,1:T(8,128)S(1)} %get-tuple-element.1662, f32[8,1,4,3,2,2,256]{6,0,5,4,3,2,1:T(8,128)S(1)} %maximum_bitcast_fusion.83, ...), kind=kOutput, calls=%fused_computation.17.clone.1 | convolution fusion | flops 80412672 | bytes 7901248 | tf_op jit(solution)/shard_map/while/body/eval_jaxpr/dot_general | solution.py:162
  111.4 100.1 %all-reduce.1 = (f32[2,16,16]{1,2,0:T(8,128)S(1)}, f32[2,16,16]{1,2,0:T(8,128)S(1)}, f32[2,16,16]{1,2,0:T(8,128)S(1)}, f32[2,16,16]{1,2,0:T(8,128)S(1)}) all-reduce(f32[2,16,16]{1,2,0:T(8,128)S(1)} %get-tuple-element.873, f32[2,16,16]{1,2,0:T(8,128)S(1)} %get-tuple-element.872, ...), channel_id=1, replica_groups=mesh['gz'=16,'ta'=32] {'gz','ta'}, use_global_device_ids=true, to_apply=%region_6.7 | all-reduce | flops 2048 | bytes 16384 | tf_op jit(solution)/shard_map/psum | solution.py:233
  211.4 0.7 copy.57
  212.1 0.7 copy.58
  212.8 0.7 copy.59
  213.5 0.7 copy.60
  (221 shorter events, 11.1 us)
Async XLA Ops:
  0.6 20.4 %copy-start.2 = (f32[4,2,2,256]{3,2,1,0:T(2,128)S(1)}, f32[4,2,2,256]{3,2,1,0:T(2,128)}, u32[]{:S(2)}) copy-start(f32[4,2,2,256]{3,2,1,0:T(2,128)} %param.9) | copy-start | bytes 49156
  0.6 20.4 %copy-start = (f32[4,18,2,2,256]{4,3,2,1,0:T(2,128)S(1)}, f32[4,18,2,2,256]{4,3,2,1,0:T(2,128)}, u32[]{:S(2)}) copy-start(f32[4,18,2,2,256]{4,3,2,1,0:T(2,128)} %param.8) | copy-start | bytes 884740
  0.7 27.0 %copy-start.3 = (s32[16]{0:T(128)S(1)}, s32[16]{0:T(128)}, u32[]{:S(2)}) copy-start(s32[16]{0:T(128)} %param.10) | copy-start | bytes 196
  4.1 27.0 %copy-start.1 = (bf16[16,2,4,3,2,2,256]{6,5,4,3,2,1,0:T(2,128)(2,1)S(1)}, bf16[16,2,4,3,2,2,256]{6,5,4,3,2,1,0:T(2,128)(2,1)}, u32[]{:S(2)}) copy-start(bf16[16,2,4,3,2,2,256]{6,5,4,3,2,1,0:T(2,128)(2,1)} %param.7) | copy-start | bytes 2359300
  4.1 26.9 %collective-permute-start = (bf16[16,2,4,3,2,1,256]{6,0,5,3,2,1,4:T(8,128)(2,1)S(1)}, bf16[16,2,4,3,2,1,256]{6,0,5,3,2,1,4:T(8,128)(2,1)S(1)}, u32[]{:S(2)}, u32[]{:S(2)}) collective-permute-start(bf16[16,2,4,3,2,1,256]{6,0,5,3,2,1,4:T(8,128)(2,1)S(1)} %copy.101), channel_id=1, source_target_pairs={{0,32},{32,64},{64,96},{96,128},{128,160},{160,192},{192,224},{224... | collective-permute-start | bytes 1179656 | tf_op jit(solution)/shard_map/ppermute | solution.py:24
  9.4 24.2 %collective-permute-start.1 = (bf16[16,2,4,3,2,1,256]{6,0,5,3,2,1,4:T(8,128)(2,1)}, bf16[16,2,4,3,2,1,256]{6,0,5,3,2,1,4:T(8,128)(2,1)}, u32[]{:S(2)}, u32[]{:S(2)}) collective-permute-start(bf16[16,2,4,3,2,1,256]{6,0,5,3,2,1,4:T(8,128)(2,1)} %copy.102), channel_id=1, source_target_pairs={{32,0},{64,32},{96,64},{128,96},{160,128},{192,160},{224,192},{256... | collective-permute-start | bytes 1179656 | tf_op jit(solution)/shard_map/ppermute | solution.py:27
  21.1 9.8 %collective-permute-start.4 = (f32[1,19,2,1,256]{4,3,2,1,0:T(1,128)S(1)}, f32[1,19,2,1,256]{4,3,2,1,0:T(1,128)S(1)}, u32[]{:S(2)}, u32[]{:S(2)}) collective-permute-start(f32[1,19,2,1,256]{4,3,2,1,0:T(1,128)S(1)} %fusion.101), channel_id=1, source_target_pairs={{0,32},{32,64},{64,96},{96,128},{128,160},{160,192},{192,224},{224... | collective-permute-start | bytes 116744 | tf_op jit(solution)/shard_map/ppermute | solution.py:15
  23.1 22.7 %collective-permute-start.5 = (f32[1,19,1,2,256]{4,3,2,1,0:T(2,128)S(1)}, f32[1,19,1,2,256]{4,3,2,1,0:T(2,128)S(1)}, u32[]{:S(2)}, u32[]{:S(2)}) collective-permute-start(f32[1,19,1,2,256]{4,3,2,1,0:T(2,128)S(1)} %fusion.102), channel_id=1, source_target_pairs={{0,1},{1,2},{2,3},{3,4},{4,5},{5,6},{6,7},{7,8},{8,9},{9,10},{10,1... | collective-permute-start | bytes 116744 | tf_op jit(solution)/shard_map/ppermute | solution.py:15
  34.7 26.3 %collective-permute-start.3 = (bf16[16,2,4,3,1,4,256]{6,0,5,3,2,1,4:T(8,128)(2,1)S(1)}, bf16[16,2,4,3,1,4,256]{6,0,5,3,2,1,4:T(8,128)(2,1)S(1)}, u32[]{:S(2)}, u32[]{:S(2)}) collective-permute-start(bf16[16,2,4,3,1,4,256]{6,0,5,3,2,1,4:T(8,128)(2,1)S(1)} %get-tuple-element.835), channel_id=1, source_target_pairs={{1,0},{2,1},{3,2},{4,3},{5,4},{6,5},{7,6},{8,7},{9,8},{10,9},{11,1... | collective-permute-start | bytes 2359304 | tf_op jit(solution)/shard_map/ppermute | solution.py:27
  43.3 18.5 %collective-permute-start.2 = (bf16[16,2,4,3,1,4,256]{6,0,5,3,2,1,4:T(8,128)(2,1)S(1)}, bf16[16,2,4,3,1,4,256]{6,0,5,3,2,1,4:T(8,128)(2,1)S(1)}, u32[]{:S(2)}, u32[]{:S(2)}) collective-permute-start(bf16[16,2,4,3,1,4,256]{6,0,5,3,2,1,4:T(8,128)(2,1)S(1)} %get-tuple-element.834), channel_id=1, source_target_pairs={{0,1},{1,2},{2,3},{3,4},{4,5},{5,6},{6,7},{7,8},{8,9},{9,10},{10,1... | collective-permute-start | bytes 2359304 | tf_op jit(solution)/shard_map/ppermute | solution.py:24
where the time goes:
time: 215 us; the launch traced here: 214 us
  blocking collectives  100 us (47%)
  starting transfers between devices  32.1 us (15%)
  other arithmetic  25 us (12%)
  matrix products  23.1 us (11%)
  waiting for transfers between devices  17.6 us (8%)
  local copies, waits for them, and re-layouts  13.9 us (6%)
    psum x1, blocking collectives, per_device(): lax.psum((one_all, two_all, one_window, two_window), ('gz', 'ta'))  100 us
    dot_general x4, matrix products, contract_time(): lax.dot_general(bra, ket, (((2, 3, 5, 6), (2, 3, 5, 6)), ((4,), (4,))), p...  23.1 us
    ppermute x2, starting transfers between devices, with_halo(): lax.ppermute(lax.slice_in_dim(block, 0, width, axis=dim), axis, backward)  20.2 us
    ppermute x2, waiting for transfers between devices, with_halo(): lax.ppermute(lax.slice_in_dim(block, 0, width, axis=dim), axis, backward)  14.2 us
    ppermute x2, starting transfers between devices, with_halo(): lax.ppermute(lax.slice_in_dim(block, block.shape[dim] - width, None, axis...  6 us
    ppermute x2, starting transfers between devices, shifted(): lax.ppermute(shard, axis, [(i, (i + by) % peers) for i in range(peers)])  5.86 us
    unnamed x15, local copies, waits for them, and re-layouts  4.38 us
  transfers between devices with their start and end apart: 6, of which 4 were waited for; matrix products, arithmetic and copies ran while one was open for 4% of the time, Pallas kernels for 0%

commit v1 on v0

v1 whole, which is shorter than its diff:
```python
import functools
import math

import jax
import jax.numpy as jnp
import numpy as np
from jax import lax
from jax.experimental import pallas as pl
from jax.experimental.pallas import tpu as pltpu
from jax.sharding import PartitionSpec as P

LY = 16
TW = 4
MODES = 16
SC = 12
SITES = 256
KETS = 192
MESH = pl.DeviceIdType.MESH

GAMMA = (
    ((3, 0, 1), (2, 0, 1), (1, 0, -1), (0, 0, -1)),
    ((3, -1, 0), (2, 1, 0), (1, 1, 0), (0, -1, 0)),
    ((2, 0, 1), (3, 0, -1), (0, 0, -1), (1, 0, 1)),
)


def fold_tables():
    space = np.zeros((2, 2, 128, 128), np.float32)
    time = np.zeros((2, 2, 2, 64, 128), np.float32)

    def put(table, column, half, mode, bra, ket, kind, sign):
        j = half * 8 + mode
        if bra == ket:
            table[column, kind * 16 + j] += sign
        elif bra == 0:
            table[column, 64 + kind * 16 + j] += sign
        else:
            table[column, 64 + kind * 16 + j] -= sign

    for bra in range(2):
        for half in range(2):
            for order in range(2):
                for part in range(2):
                    for ket in range(2):
                        for mode in range(8):
                            low = part * 16 + ket * 8 + mode
                            s_col = (order * 2) * 32 + low
                            d_col = (order * 2 + 1) * 32 + low
                            t_col = order * 32 + low
                            f, b = order * 2, order * 2 + 1
                            put(space[bra, half], s_col, half, mode, bra, ket, f, 1)
                            put(space[bra, half], s_col, half, mode, bra, ket, b, 1)
                            put(space[bra, half], d_col, half, mode, bra, ket, f, -1)
                            put(space[bra, half], d_col, half, mode, bra, ket, b, 1)
                            put(time[0, bra, half], t_col, half, mode, bra, ket, f, 1)
                            put(time[0, bra, half], t_col, half, mode, bra, ket, b, 1)
                            put(time[1, bra, half], t_col, half, mode, bra, ket, f, -1)
                            put(time[1, bra, half], t_col, half, mode, bra, ket, b, 1)
    return space.reshape(512, 128), time.reshape(512, 128)


def split(value):
    high = value.astype(jnp.bfloat16)
    low = (value - high.astype(jnp.float32)).astype(jnp.bfloat16)
    return high, low


def colour_row(rows, vectors):
    result = []
    for spin in range(4):
        total_re = None
        total_im = None
        for b in range(3):
            ur, ui = rows[b]
            value = vectors(spin * 3 + b)
            vr, vi = value[:8], value[8:]
            re = ur * vr - ui * vi
            im = ur * vi + ui * vr
            total_re = re if total_re is None else total_re + re
            total_im = im if total_im is None else total_im + im
        result.append((total_re, total_im))
    return result


def times(entry, pair):
    _, re, im = entry
    if re:
        return (re, pair[0]), (re, pair[1])
    return (-im, pair[1]), (im, pair[0])


def add_signed(total, sign, value):
    if total is None:
        return value if sign > 0 else -value
    return total + value if sign > 0 else total - value


def vector_unit(block_t, block_z, lane, half, vall, vxy, links, field, ket):
    rows16 = pl.ds(half * 16, 16)
    lanes = pl.ds(pl.multiple_of(lane * 128, 128), 128)
    lanes_y = pl.ds(pl.multiple_of(256 + lane * 128, 128), 128)

    def from_x(sc):
        return vxy[pl.ds(sc * 32 + half * 16, 16), lanes]

    def from_y(sc):
        return vxy[pl.ds(sc * 32 + half * 16, 16), lanes_y]

    def from_z(sc):
        return vall[block_t, block_z + 1, sc, rows16, lanes].astype(jnp.float32)

    def from_t(sc):
        return vall[block_t + 1, block_z, sc, rows16, lanes].astype(jnp.float32)

    sources = (from_x, from_y, from_z, from_t)

    def store(kind_row, sc, pair):
        high, low = split(jnp.concatenate(pair, axis=0))
        ket[pl.ds(kind_row, 16), pl.ds(sc * 128, 128)] = high
        ket[pl.ds(kind_row + 16, 16), pl.ds(sc * 128, 128)] = low

    for a in range(3):
        sums = [[[None, None] for _ in range(4)] for _ in range(4)]
        for mu in range(4):
            rows = [
                (
                    links[block_t, block_z, mu * 18 + a * 3 + b, :, lanes],
                    links[block_t, block_z, mu * 18 + 9 + a * 3 + b, :, lanes],
                )
                for b in range(3)
            ]
            photon = field[block_t, block_z, mu, :, lanes]
            first = colour_row(rows, sources[mu])
            second = [(photon * re, photon * im) for re, im in first]
            if mu == 3:
                for spin in range(4):
                    store(128, spin * 3 + a, first[spin])
                    store(160, spin * 3 + a, second[spin])
                continue
            for order, hopped in enumerate((first, second)):
                for spin in range(4):
                    plain = sums[order * 2][spin]
                    crossed = sums[order * 2 + 1][spin]
                    entry = GAMMA[mu][spin]
                    turned = times(entry, hopped[entry[0]])
                    for part in range(2):
                        plain[part] = add_signed(plain[part], 1, hopped[spin][part])
                        crossed[part] = add_signed(crossed[part], *turned[part])
        for kind in range(4):
            for spin in range(4):
                store(kind * 32, spin * 3 + a, sums[kind][spin])


def product_unit(block_t, block_z, lane, half, vall, ket, acc):
    lanes = pl.ds(pl.multiple_of(lane * 128, 128), 128)
    pieces = [vall[block_t, block_z, sc, :, lanes] for sc in range(SC)]
    bra = jnp.concatenate(
        [
            jnp.concatenate(pieces, axis=1),
            jnp.concatenate(pieces[6:] + pieces[:6], axis=1),
        ],
        axis=0,
    )
    acc[block_t, half] += lax.dot_general(
        bra, ket[...], (((1,), (1,)), ((), ())), preferred_element_type=jnp.float32
    )


def hop_kernel(
    counts,
    comm,
    start_ref,
    low_ref,
    link_ref,
    photon_ref,
    space_ref,
    time_ref,
    out_ref,
    vall,
    vxy,
    perm,
    links,
    field,
    ket_a,
    ket_b,
    acc,
    slots,
    local_sem,
    send_sem,
    recv_sem,
    sum_send,
    sum_recv,
):
    n_gz, n_ta = counts
    if comm:
        gz, ta = lax.axis_index("gz"), lax.axis_index("ta")
    else:
        gz, ta = 0, 0

    def at(g, t):
        return {"gz": g, "ta": t}

    z_hi, x = gz // 4, gz % 4
    y, z_lo, core = ta // 4, (ta // 2) % 2, ta % 2
    z = z_hi * 2 + z_lo

    def group_a(index):
        return at(z_hi * 4 + index // 2, y * 4 + z_lo * 2 + index % 2)

    def group_b(index):
        return at((index // 2) * 4 + x, y * 4 + (index % 2) * 2 + core)

    def group_c(index):
        return at(gz, index * 4 + z_lo * 2 + core)

    stages = ((group_a, x * 2 + core), (group_b, z), (group_c, y))
    below_z = at((gz + n_gz - 1) % n_gz, ta)
    above_z = at((gz + 1) % n_gz, ta)
    below_t = at(gz, (ta + n_ta - 1) % n_ta)
    above_t = at(gz, (ta + 1) % n_ta)

    barrier = pltpu.get_barrier_semaphore() if comm else None
    if comm:
        for device in (below_z, above_z, below_t, above_t):
            pl.semaphore_signal(barrier, inc=1, device_id=device, device_id_type=MESH)
        for group, index in stages:
            for step in range(1, 8):
                pl.semaphore_signal(
                    barrier, inc=1, device_id=group((index + step) % 8), device_id_type=MESH
                )

    own = [
        pltpu.make_async_copy(low_ref.at[t, zz], vall.at[t, zz], local_sem.at[t * 2 + zz])
        for t in range(2)
        for zz in range(2)
    ]
    for copy in own:
        copy.start()

    def halo(src, dst, which, device):
        if comm:
            return pltpu.make_async_remote_copy(
                src_ref=low_ref.at[src],
                dst_ref=vall.at[dst],
                send_sem=send_sem.at[which],
                recv_sem=recv_sem.at[which],
                device_id=device,
                device_id_type=MESH,
            )
        return pltpu.make_async_copy(low_ref.at[src], vall.at[dst], recv_sem.at[which])

    halos = [
        halo((0, 0), (2, 0), 0, below_t),
        halo((0, 0), (0, 2), 1, below_z),
        halo((0, 1), (2, 1), 2, below_t),
        halo((1, 0), (1, 2), 3, below_z),
    ]

    if comm:
        pl.semaphore_wait(barrier, 25)
    for copy in halos:
        copy.start()

    row = lax.broadcasted_iota(jnp.int32, (SITES, SITES), 0)
    column = lax.broadcasted_iota(jnp.int32, (SITES, SITES), 1)
    along_x = (column + LY) % SITES
    along_y = (column - column % LY) + (column + 1) % LY
    perm[:, :SITES] = (row == along_x).astype(jnp.float32).astype(jnp.bfloat16)
    perm[:, SITES:] = (row == along_y).astype(jnp.float32).astype(jnp.bfloat16)

    def spread(t, _):
        edge = jnp.where(jnp.logical_and(ta == n_ta - 1, t == 1), -1.0, 1.0)
        for mu in range(4):
            photon = photon_ref[mu, t]
            scale = photon * edge if mu == 3 else photon
            for zz in range(2):
                field[t, zz, mu] = jnp.broadcast_to(photon[zz : zz + 1], (8, SITES))
            for entry in range(18):
                scaled = link_ref[mu, entry, t] * scale
                for zz in range(2):
                    links[t, zz, mu * 18 + entry] = jnp.broadcast_to(
                        scaled[zz : zz + 1], (8, SITES)
                    )
        return 0

    lax.fori_loop(0, 2, spread, 0)

    acc[...] = jnp.zeros_like(acc)
    ket_b[...] = jnp.zeros_like(ket_b)
    for copy in own:
        copy.wait()

    def step(index, _):
        block = index // 2
        lane = index % 2
        block_t, block_z = block % 2, block // 2
        before = jnp.maximum(index - 1, 0)
        before_block = before // 2
        before_t, before_z, before_lane = before_block % 2, before_block // 2, before % 2

        @pl.when(lane == 0)
        def _():
            for which, number in ((0, 1), (1, 2), (2, 3), (3, 3)):
                @pl.when(block == number)
                def _(which=which):
                    halos[which].wait_recv() if comm else halos[which].wait()

            vxy[...] = jnp.dot(
                vall[block_t, block_z].reshape(SC * 32, SITES),
                perm[...],
                preferred_element_type=jnp.float32,
            )

        product_unit(before_t, before_z, before_lane, 1, vall, ket_b, acc)
        vector_unit(block_t, block_z, lane, 0, vall, vxy, links, field, ket_a)
        product_unit(block_t, block_z, lane, 0, vall, ket_a, acc)
        vector_unit(block_t, block_z, lane, 1, vall, vxy, links, field, ket_b)
        return 0

    lax.fori_loop(0, 8, step, 0)
    product_unit(1, 1, 1, 1, vall, ket_b, acc)

    def bra_rows(values, swapped, part):
        base = swapped * 32 + part * 8
        return jnp.concatenate([values[base : base + 8], values[base + 16 : base + 24]], axis=0)

    total = jnp.zeros((MODES, 128), jnp.float32)
    inside_total = jnp.zeros((MODES, 128), jnp.float32)
    lattice_t = 2 * n_ta
    begin = start_ref[0]
    kind = lax.broadcasted_iota(jnp.int32, (1, 128), 1) // 16 % 2

    def inside(t):
        offset = (t - begin + 2 * lattice_t) % lattice_t
        return jnp.where(offset < TW, 1.0, 0.0)

    for t in range(2):
        space_sum = jnp.zeros((MODES, 128), jnp.float32)
        time_sum = jnp.zeros((MODES, 128), jnp.float32)
        for half in range(2):
            values = acc[t, half]
            for part in range(2):
                table = space_ref[pl.ds((part * 2 + half) * 128, 128), :]
                space_sum += jnp.dot(
                    bra_rows(values, 0, part)[:, :128],
                    table,
                    precision=lax.Precision.HIGHEST,
                    preferred_element_type=jnp.float32,
                )
                for swapped in range(2):
                    table = time_ref[pl.ds(((swapped * 2 + part) * 2 + half) * 64, 64), :]
                    time_sum += jnp.dot(
                        bra_rows(values, swapped, part)[:, 128:],
                        table,
                        precision=lax.Precision.HIGHEST,
                        preferred_element_type=jnp.float32,
                    )
        here = inside(ta * 2 + t)
        after = inside(ta * 2 + t + 1)
        total += space_sum + time_sum
        inside_total += here * space_sum + jnp.where(kind == 0, here, after) * time_sum

    value = jnp.concatenate([total, inside_total], axis=0)
    if comm:
        for number, (group, index) in enumerate(stages):
            slots[number, index] = value
            copies = []
            for hop in range(1, 8):
                copy = pltpu.make_async_remote_copy(
                    src_ref=slots.at[number, index],
                    dst_ref=slots.at[number, index],
                    send_sem=sum_send.at[number, hop],
                    recv_sem=sum_recv.at[number, index],
                    device_id=group((index + hop) % 8),
                    device_id_type=MESH,
                )
                copy.start()
                copies.append(copy)
            for hop in range(1, 8):
                peer = (index + hop) % 8
                pltpu.make_async_remote_copy(
                    src_ref=slots.at[number, peer],
                    dst_ref=slots.at[number, peer],
                    send_sem=sum_send.at[number, hop],
                    recv_sem=sum_recv.at[number, peer],
                    device_id=group(peer),
                    device_id_type=MESH,
                ).wait_recv()
            value = slots[number, 0]
            for other in range(1, 8):
                value = value + slots[number, other]
            for copy in copies:
                copy.wait_send()
        for copy in halos:
            copy.wait_send()
    out_ref[...] = value.reshape(2, MODES, 128)


def insert_sums(counts, comm, low, links, photon, start):
    space, time = fold_tables()
    vmem = pl.BlockSpec(memory_space=pltpu.VMEM)
    return pl.pallas_call(
        functools.partial(hop_kernel, counts, comm),
        out_shape=jax.ShapeDtypeStruct((2, MODES, 128), jnp.float32),
        in_specs=[
            pl.BlockSpec(memory_space=pltpu.SMEM),
            pl.BlockSpec(memory_space=pl.ANY),
            vmem,
            vmem,
            vmem,
            vmem,
        ],
        out_specs=vmem,
        scratch_shapes=[
            pltpu.VMEM((3, 3, SC, 32, SITES), jnp.bfloat16),
            pltpu.VMEM((SC * 32, 2 * SITES), jnp.float32),
            pltpu.VMEM((SITES, 2 * SITES), jnp.bfloat16),
            pltpu.VMEM((2, 2, 72, 8, SITES), jnp.float32),
            pltpu.VMEM((2, 2, 4, 8, SITES), jnp.float32),
            pltpu.VMEM((KETS, SC * 128), jnp.bfloat16),
            pltpu.VMEM((KETS, SC * 128), jnp.bfloat16),
            pltpu.VMEM((2, 2, 64, KETS), jnp.float32),
            pltpu.VMEM((3, 8, 2 * MODES, 128), jnp.float32),
            pltpu.SemaphoreType.DMA((4,)),
            pltpu.SemaphoreType.DMA((4,)),
            pltpu.SemaphoreType.DMA((4,)),
            pltpu.SemaphoreType.DMA((3, 8)),
            pltpu.SemaphoreType.DMA((3, 8)),
        ],
        compiler_params=pltpu.CompilerParams(
            collective_id=0 if comm else None,
            has_side_effects=comm,
            vmem_limit_bytes=32 * 1024 * 1024,
        ),
    )(start, low, links, photon, jnp.asarray(space), jnp.asarray(time))


def per_device(counts, comm, low_modes, gauge_links, photon, charges, window_start):
    n_gz, n_ta = counts
    low = low_modes.reshape(2, 8, 2, SC, 2, 2, SITES)
    low = low.transpose(4, 5, 3, 0, 2, 1, 6).reshape(2, 2, SC, 32, SITES)
    sums = insert_sums(counts, comm, low, gauge_links, photon, window_start)
    sums = sums.reshape(2, MODES, 2, 4, MODES)
    charge = charges.astype(jnp.float32) / 3.0
    lattice = 24.0 * SITES * (2 * n_gz)
    scales = (1.0 / math.sqrt(lattice * 2 * n_ta), 1.0 / math.sqrt(lattice * TW))
    outputs = []
    for window in range(2):
        for order in range(2):
            f_re = sums[window, :, 0, 2 * order]
            f_im = sums[window, :, 1, 2 * order]
            b_re = sums[window, :, 0, 2 * order + 1].T
            b_im = -sums[window, :, 1, 2 * order + 1].T
            if order == 0:
                factor = 0.5 * scales[window] * charge
                outputs.append(jnp.stack([(f_im - b_im) * factor, -(f_re - b_re) * factor]))
            else:
                factor = 0.25 * scales[window] * charge * charge
                outputs.append(jnp.stack([(f_re + b_re) * factor, (f_im + b_im) * factor]))
    return tuple(outputs)


def solution(mesh):
    counts = (mesh.shape["gz"], mesh.shape["ta"])
    return jax.shard_map(
        functools.partial(per_device, counts, True),
        mesh=mesh,
        in_specs=(
            P(None, None, None, None, "ta", "gz", None),
            P(None, None, "ta", "gz", None),
            P(None, "ta", "gz", None),
            P(),
            P(),
        ),
        out_specs=(P(), P(), P(), P()),
        check_vma=False,
    )
```

time: 215 us -> 62.7 us (0.29)
  blocking collectives: 100 us -> 0 us
  Pallas kernels: 0 us -> 55.6 us
  starting transfers between devices: 32.1 us -> 0 us
  matrix products: 23.1 us -> 0 us
  other arithmetic: 25 us -> 2.46 us
  waiting for transfers between devices: 17.6 us -> 0 us
  local copies, waits for them, and re-layouts: 13.9 us -> 3.11 us
    psum x1 -> x0, blocking collectives: 100 us -> none  [per_device(): lax.psum((one_all, two_all, one_window, two_window), ('gz', 'ta'))]
    pallas_call x0 -> x1, Pallas kernels: none -> 55.6 us  [insert_sums(): pl.pallas_call(functools.partial(hop_kernel, counts, comm), out_shape=jax...]
    ppermute x6 -> x0, starting transfers between devices: 32.1 us -> none  [the longest x2 20.2 us: with_halo(): lax.ppermute(lax.slice_in_dim(block, 0, width, axis=dim), axis, backward)]
    dot_general x4 -> x0, matrix products: 23.1 us -> none  [contract_time(): lax.dot_general(bra, ket, (((2, 3, 5, 6), (2, 3, 5, 6)), ((4,), (4,))), p...]
    ppermute x6 -> x0, waiting for transfers between devices: 17.6 us -> none  [the longest x2 14.2 us: with_halo(): lax.ppermute(lax.slice_in_dim(block, 0, width, axis=dim), axis, backward)]
    slice x18 -> x1, local copies, waits for them, and re-layouts: 6.25 us -> 0.1 us  [per_device(): b_re = sums[window, :, 0, 2 * order + 1].T]
    convert_element_type x5 -> x0, other arithmetic: 5.85 us -> none  [the longest x2 3.6 us: insert_block(): values = padded.astype(jnp.float32)]
    sub x46 -> x0, other arithmetic: 5.32 us -> none  [the longest x28 3.06 us: color_apply(): sum_real = sum_real + link_real * part_real - link_imag * part_imag]
  transfers between devices with their start and end apart: 6 -> 0, of which waited for: 4 -> 0; matrix products, arithmetic and copies ran while one was open for 4% -> 0% of each run, Pallas kernels for 0% -> 0%
where the time goes in v1:
time: 62.7 us; the launch traced here: 62.6 us
  Pallas kernels  55.6 us (89%)
  local copies, waits for them, and re-layouts  3.11 us (5%)
  other arithmetic  2.46 us (4%)
  between operations  1.38 us (2%)
    pallas_call x1, Pallas kernels, insert_sums(): pl.pallas_call(functools.partial(hop_kernel, counts, comm), out_shape=jax...  55.6 us
    reshape x1, local copies, waits for them, and re-layouts, per_device(): low = low_modes.reshape(2, 8, 2, SC, 2, 2, SITES)  1.64 us

profile of v1, /device:TPU:1, one launch (start us, length us, event | category | flops | bytes accessed | tf_op | source)
XLA Modules:
  0.0 62.6 jit_solution(18182171634185095125)
XLA Ops:
  0.6 0.0 copy-start
  0.6 0.0 copy-start.1
  0.7 0.0 copy-start.2
  0.7 0.0 copy-start.3
  0.7 1.6 %copy.11 = bf16[2,8,2,12,2,2,256]{6,1,2,0,3,5,4:T(8,128)(2,1)S(1)} copy(bf16[2,8,2,12,2,2,256]{6,5,4,3,2,1,0:T(2,128)(2,1)} %bitcast.113) | data formatting | bytes 1572864 | tf_op jit(solution)/shard_map/reshape | solution.py:440
  3.0 0.0 copy-done
  3.0 0.0 copy-done.1
  3.0 0.0 copy-done.2
  3.0 0.0 copy-done.3
  3.0 55.6 %shard_map.102 = f32[2,16,128]{2,1,0:T(8,128)S(1)} custom-call(s32[1]{0:T(128)S(6)} %copy.44.start_ref, bf16[2,2,12,32,256]{4,3,2,1,0:T(8,128)(2,1)S(1)} %bitcast.112, f32[4,18,2,2,256]{4,3,2,1,0:T(2,128)S(1)} %copy-done, f32[4,2,2,256]{3,2,1,0:T(2,128)S(1)} %copy-done.3, f32[512,128]{1,0:T(8,128)S(1)} %copy-done.1, f32[512,128]{1,0:T(8,128)S(1)} %copy-done.2), custom_call_target="tpu_custom_call" | custom-call | tf_op jit(solution)/shard_map/pallas_call | solution.py:402
  58.6 0.1 reshape.27
  58.8 0.1 fusion.18
  58.9 0.1 copy.37
  58.9 0.1 copy.39
  59.0 0.1 copy.41
  59.1 0.1 copy.43
  59.1 0.0 copy-start.4
  59.1 0.7 %copy-done.4 = s32[16]{0:T(128)S(1)} copy-done((s32[16]{0:T(128)S(1)}, s32[16]{0:T(128)}, u32[]{:S(2)}) %copy-start.4) | copy-done | bytes 88
  59.8 0.6 pad_maximum_fusion.3
  60.4 0.6 pad_maximum_fusion.2
  61.0 0.1 copy.29
  61.1 0.1 copy.31
  61.2 0.1 copy.33
  61.2 0.1 copy.35
  61.3 0.6 pad_maximum_fusion.1
  61.9 0.6 pad_maximum_fusion
  (3 shorter events, 0.0 us)
Async XLA Ops:
  0.6 2.3 %copy-start = (f32[4,18,2,2,256]{4,3,2,1,0:T(2,128)S(1)}, f32[4,18,2,2,256]{4,3,2,1,0:T(2,128)}, u32[]{:S(2)}) copy-start(f32[4,18,2,2,256]{4,3,2,1,0:T(2,128)} %link_ref.1) | copy-start | bytes 884740
  0.6 2.3 %copy-start.1 = (f32[512,128]{1,0:T(8,128)S(1)}, f32[512,128]{1,0:T(8,128)}, u32[]{:S(2)}) copy-start(f32[512,128]{1,0:T(8,128)} %constant.19.clone.space_ref) | copy-start | bytes 786436
  0.7 2.3 %copy-start.2 = (f32[512,128]{1,0:T(8,128)S(1)}, f32[512,128]{1,0:T(8,128)}, u32[]{:S(2)}) copy-start(f32[512,128]{1,0:T(8,128)} %constant.20.clone.time_ref) | copy-start | bytes 786436
  0.7 2.3 %copy-start.3 = (f32[4,2,2,256]{3,2,1,0:T(2,128)S(1)}, f32[4,2,2,256]{3,2,1,0:T(2,128)}, u32[]{:S(2)}) copy-start(f32[4,2,2,256]{3,2,1,0:T(2,128)} %photon_ref.1) | copy-start | bytes 49156
  59.1 0.7 %copy-start.4 = (s32[16]{0:T(128)S(1)}, s32[16]{0:T(128)}, u32[]{:S(2)}) copy-start(s32[16]{0:T(128)} %param.10) | copy-start | bytes 196

commit v2 on v1

v2 whole, which is shorter than its diff:
```python
import functools
import math

import jax
import jax.numpy as jnp
import numpy as np
from jax import lax
from jax.experimental import pallas as pl
from jax.experimental.pallas import tpu as pltpu
from jax.sharding import PartitionSpec as P

LY = 16
TW = 4
MODES = 16
SC = 12
SITES = 256
ROWS = SC * 32
EDGE = 24
MESH = pl.DeviceIdType.MESH

GAMMA = (
    ((3, 0, 1), (2, 0, 1), (1, 0, -1), (0, 0, -1)),
    ((3, -1, 0), (2, 1, 0), (1, 1, 0), (0, -1, 0)),
    ((2, 0, 1), (3, 0, -1), (0, 0, -1), (1, 0, 1)),
)


def fold_table():
    table = np.zeros((1536, 128), np.float32)

    def put(row, ket, order, plain, value):
        for side in range(2):
            factor = value * (0.5 if order == 0 else 0.25)
            if side == 0:
                factor = factor if plain else -factor
                factor = factor * (-1j if order == 0 else 1)
                parts = (factor.real, factor.imag)
            else:
                factor = np.conj(factor) * (1j if order == 0 else 1)
                parts = (factor.real, factor.imag)
            for part in range(2):
                table[row, side * 64 + part * 32 + order * 16 + ket] += parts[part]

    for bra in range(2):
        for half in range(2):
            for low in range(2):
                for part in range(2):
                    for mode in range(8):
                        ket = half * 8 + mode
                        value = (1, -1j)[bra] * (1, 1j)[part]
                        tail = low * 16 + part * 8 + mode
                        for kind in range(4):
                            row = bra * 256 + half * 128 + kind * 32 + tail
                            put(row, ket, kind // 2, kind % 2 == 0, value)
                        for order in range(2):
                            for turned in range(2):
                                row = (turned * 2 + bra) * 128 + half * 64 + order * 32 + tail
                                put(512 + row, ket, order, turned == 0, value)
                                phase = 1j if turned else 1
                                put(1024 + row, ket, order, turned == 0, value * phase)
    return table


def split(value):
    high = value.astype(jnp.bfloat16)
    low = (value - high.astype(jnp.float32)).astype(jnp.bfloat16)
    return high, low


def colour_row(rows, vectors):
    result = []
    for spin in range(4):
        total_re = None
        total_im = None
        for b in range(3):
            ur, ui = rows[b]
            value = vectors(spin * 3 + b)
            vr, vi = value[:8], value[8:]
            re = ur * vr - ui * vi
            im = ur * vi + ui * vr
            total_re = re if total_re is None else total_re + re
            total_im = im if total_im is None else total_im + im
        result.append((total_re, total_im))
    return result


def times(entry, pair):
    _, re, im = entry
    if re:
        return (re, pair[0]), (re, pair[1])
    return (-im, pair[1]), (im, pair[0])


def add_signed(total, sign, value):
    if total is None:
        return value if sign > 0 else -value
    return total + value if sign > 0 else total - value


def link_rows(links, slot, base, a, lanes):
    return [
        (links[slot, base + a * 3 + b, :, lanes], links[slot, base + 9 + a * 3 + b, :, lanes])
        for b in range(3)
    ]


def store_pair(ket, row, column, pair):
    high, low = split(jnp.concatenate(pair, axis=0))
    ket[row : row + 16, column : column + 128] = high
    ket[row + 16 : row + 32, column : column + 128] = low


def space_unit(t, zz, lane, half, vall, vxy, links, field, ket):
    lanes = slice(lane * 128, lane * 128 + 128)
    slot = t * 2 + zz

    def from_x(sc):
        return vxy[sc * 32 + half * 16 : sc * 32 + half * 16 + 16, lanes]

    def from_y(sc):
        row = sc * 32 + half * 16
        return vxy[row : row + 16, SITES + lane * 128 : SITES + lane * 128 + 128]

    def from_z(sc):
        rows = slice(half * 16, half * 16 + 16)
        return vall[t + 1, zz + 2, sc, rows, lanes].astype(jnp.float32)

    sources = (from_x, from_y, from_z) if zz == 0 else (from_x, from_y)
    for a in range(3):
        sums = [[[None, None] for _ in range(4)] for _ in range(4)]
        for mu, source in enumerate(sources):
            first = colour_row(link_rows(links, slot, mu * 18, a, lanes), source)
            photon = field[slot, mu, :, lanes]
            second = [(photon * re, photon * im) for re, im in first]
            for order, hopped in enumerate((first, second)):
                for spin in range(4):
                    plain = sums[order * 2][spin]
                    crossed = sums[order * 2 + 1][spin]
                    entry = GAMMA[mu][spin]
                    turned = times(entry, hopped[entry[0]])
                    for part in range(2):
                        plain[part] = add_signed(plain[part], 1, hopped[spin][part])
                        crossed[part] = add_signed(crossed[part], *turned[part])
        for kind in range(4):
            for spin in range(4):
                store_pair(ket, half * 128 + kind * 32, (spin * 3 + a) * 128, sums[kind][spin])


def space_product(t, zz, lane, vall, ket):
    lanes = slice(lane * 128, lane * 128 + 128)
    bra = jnp.concatenate([vall[t + 1, zz + 1, sc, :, lanes] for sc in range(SC)], axis=1)
    return lax.dot_general(
        bra, ket[...], (((1,), (1,)), ((), ())), preferred_element_type=jnp.float32
    )


def link_unit(up, slot, mu, lane, half, vall, links, field, ket):
    lanes = slice(lane * 128, lane * 128 + 128)

    def source(sc):
        return vall[up[0], up[1], sc, half * 16 : half * 16 + 16, lanes].astype(jnp.float32)

    photon = field[slot, mu, :, lanes]
    for a in range(3):
        first = colour_row(link_rows(links, slot, mu * 18, a, lanes), source)
        for spin in range(4):
            re, im = first[spin]
            column = (spin * 3 + a) * SITES + lane * 128
            store_pair(ket, half * 64, column, (re, im))
            store_pair(ket, half * 64 + 32, column, (photon * re, photon * im))


def link_product(low, sign, vall, ket):
    pieces = [vall[low[0], low[1], sc] for sc in range(SC)]
    turned = [pieces[(sc + 6) % SC] for sc in range(SC)]
    turned = [piece * sign if sc // 3 in (0, 3) else piece for sc, piece in enumerate(turned)]
    bra = jnp.concatenate(
        [jnp.concatenate(pieces, axis=1), jnp.concatenate(turned, axis=1)], axis=0
    )
    return lax.dot_general(
        bra, ket[...], (((1,), (1,)), ((), ())), preferred_element_type=jnp.float32
    )


def hop_kernel(
    counts,
    comm,
    start_ref,
    charge_ref,
    low_ref,
    link_ref,
    photon_ref,
    table_ref,
    out_ref,
    vall,
    vxy_a,
    vxy_b,
    perm,
    links,
    field,
    edge_out,
    edge_in,
    ket_s0,
    ket_s1,
    ket_p0,
    ket_p1,
    acc_s,
    acc_p,
    slots,
    local_sem,
    send_sem,
    recv_sem,
    sum_send,
    sum_recv,
):
    n_gz, n_ta = counts
    if comm:
        gz, ta = lax.axis_index("gz"), lax.axis_index("ta")
    else:
        gz, ta = jnp.int32(0), jnp.int32(0)

    def at(g, t):
        return {"gz": g, "ta": t}

    z_hi, x = gz // 4, gz % 4
    y, z_lo, core = ta // 4, (ta // 2) % 2, ta % 2
    z = z_hi * 2 + z_lo

    def group_a(index):
        return at(z_hi * 4 + index // 2, y * 4 + z_lo * 2 + index % 2)

    def group_b(index):
        return at((index // 2) * 4 + x, y * 4 + (index % 2) * 2 + core)

    def group_c(index):
        return at(gz, index * 4 + z_lo * 2 + core)

    stages = ((group_a, x * 2 + core), (group_b, z), (group_c, y))
    below_z = at((gz + n_gz - 1) % n_gz, ta)
    above_z = at((gz + 1) % n_gz, ta)
    below_t = at(gz, (ta + n_ta - 1) % n_ta)
    above_t = at(gz, (ta + 1) % n_ta)

    first_kind = z_lo == 0
    upper_up = jnp.logical_and(
        core == 1,
        jnp.logical_or(
            jnp.logical_and(x == 0, first_kind),
            jnp.logical_and(x == 3, jnp.logical_not(first_kind)),
        ),
    )
    lower_up = jnp.logical_and(
        core == 0,
        jnp.logical_or(
            jnp.logical_and(x == 0, jnp.logical_not(first_kind)),
            jnp.logical_and(x == 3, first_kind),
        ),
    )
    upper_down = jnp.logical_not(upper_up)
    lower_down = jnp.logical_not(lower_up)
    always = None

    barrier = pltpu.get_barrier_semaphore() if comm else None
    if comm:
        for device in (below_z, above_z, below_t, above_t):
            pl.semaphore_signal(barrier, inc=1, device_id=device, device_id_type=MESH)
        for group, index in stages:
            for step in range(1, 8):
                pl.semaphore_signal(
                    barrier, inc=1, device_id=group((index + step) % 8), device_id_type=MESH
                )

    own = [
        pltpu.make_async_copy(
            low_ref.at[t, zz], vall.at[t + 1, zz + 1], local_sem.at[t * 2 + zz]
        )
        for t in range(2)
        for zz in range(2)
    ]
    for copy in own:
        copy.start()

    def copy_to(src, dst, which, device):
        if comm:
            return pltpu.make_async_remote_copy(
                src_ref=src,
                dst_ref=dst,
                send_sem=send_sem.at[which],
                recv_sem=recv_sem.at[which],
                device_id=device,
                device_id_type=MESH,
            )
        return pltpu.make_async_copy(src, dst, recv_sem.at[which])

    down_z = (copy_to(low_ref.at[0, 0], vall.at[1, 3], 0, below_z), always, always)
    up_z = (copy_to(low_ref.at[1, 1], vall.at[2, 0], 1, above_z), always, always)
    down_t = [
        (copy_to(low_ref.at[0, zz], vall.at[3, zz + 1], 2 + zz, below_t), lower_down, upper_down)
        for zz in range(2)
    ]
    up_t = [
        (copy_to(low_ref.at[1, zz], vall.at[0, zz + 1], 4 + zz, above_t), upper_up, lower_up)
        for zz in range(2)
    ]
    edge_z = (copy_to(edge_out.at[0], edge_in.at[0], 6, above_z), always, always)
    edge_t = (
        copy_to(edge_out.at[pl.ds(1, 2)], edge_in.at[pl.ds(1, 2)], 7, above_t),
        upper_up,
        lower_up,
    )

    def guarded(flag, action):
        if flag is None:
            action()
        else:
            pl.when(flag)(action)

    def start(item):
        guarded(item[1], item[0].start)

    def arrive(item):
        guarded(item[2], item[0].wait_recv if comm else item[0].wait)

    if comm:
        pl.semaphore_wait(barrier, 25)
    for item in (down_z, up_z, *down_t, *up_t):
        start(item)

    def spread(t, _):
        turn = jnp.where(jnp.logical_and(ta == n_ta - 1, t == 1), -1.0, 1.0)
        for mu in range(4):
            photon = photon_ref[mu, t]
            scale = photon * turn if mu == 3 else photon
            for zz in range(2):
                field[t * 2 + zz, mu] = jnp.broadcast_to(photon[zz : zz + 1], (8, SITES))
            for entry in range(18):
                scaled = link_ref[mu, entry, t] * scale
                for zz in range(2):
                    links[t * 2 + zz, mu * 18 + entry] = jnp.broadcast_to(
                        scaled[zz : zz + 1], (8, SITES)
                    )
        return 0

    lax.fori_loop(0, 2, spread, 0)

    for number, (slot, mu) in enumerate(((3, 2), (2, 3), (3, 3))):
        rows = [links[slot, mu * 18 + entry, 0:1] for entry in range(18)]
        rows.append(field[slot, mu, 0:1])
        rows.append(jnp.zeros((EDGE - 19, SITES), jnp.float32))
        edge_out[number] = jnp.concatenate(rows, axis=0)
    start(edge_z)
    start(edge_t)

    row = lax.broadcasted_iota(jnp.int32, (SITES, SITES), 0)
    column = lax.broadcasted_iota(jnp.int32, (SITES, SITES), 1)
    along_x = (column + LY) % SITES
    along_y = (column - column % LY) + (column + 1) % LY
    perm[:, :SITES] = (row == along_x).astype(jnp.float32).astype(jnp.bfloat16)
    perm[:, SITES:] = (row == along_y).astype(jnp.float32).astype(jnp.bfloat16)

    acc_p[...] = jnp.zeros_like(acc_p)
    for copy in own:
        copy.wait()

    def shift(t, zz, vxy):
        vxy[...] = jnp.dot(
            vall[t + 1, zz + 1].reshape(ROWS, SITES),
            perm[...],
            preferred_element_type=jnp.float32,
        )

    shift(0, 0, vxy_a)

    def blocks(t, _):
        kets = (ket_s0, ket_s1)
        total = None
        pending = None
        for zz, vxy in ((0, vxy_a), (1, vxy_b)):
            if zz == 0:
                shift(t, 1, vxy_b)
            for lane in range(2):
                if pending is not None:
                    product = space_product(t, *pending, vall, kets[pending[1]])
                    total = product if total is None else total + product
                for half in range(2):
                    space_unit(t, zz, lane, half, vall, vxy, links, field, kets[lane])
                pending = (zz, lane)
            if zz == 0:
                shift(jnp.minimum(t + 1, 1), 0, vxy_a)
        acc_s[t] = total + space_product(t, *pending, vall, kets[pending[1]])
        return 0

    lax.fori_loop(0, 2, blocks, 0)

    def spread_edge(number, slot, mu):
        for entry in range(18):
            links[slot, mu * 18 + entry] = jnp.broadcast_to(
                edge_in[number, entry : entry + 1], (8, SITES)
            )
        field[slot, mu] = jnp.broadcast_to(edge_in[number, 18:19], (8, SITES))

    def pair(number, _):
        is_z = number == 3

        @pl.when(number == 1)
        def _():
            arrive(down_t[0])
            arrive(down_t[1])

        @pl.when(number == 2)
        def _():
            arrive(up_t[0])
            arrive(up_t[1])
            arrive(edge_t)

            @pl.when(lower_up)
            def _():
                spread_edge(1, 5, 3)
                spread_edge(2, 6, 3)

        @pl.when(is_z)
        def _():
            arrive(down_z)
            arrive(up_z)
            arrive(edge_z)
            spread_edge(0, 4, 2)

        active = jnp.logical_or(
            jnp.logical_or(number == 0, is_z),
            jnp.logical_or(
                jnp.logical_and(number == 1, upper_down), jnp.logical_and(number == 2, lower_up)
            ),
        )

        @pl.when(active)
        def _():
            mu = jnp.where(is_z, 2, 3)
            sign = jnp.where(is_z, -1.0, 1.0).astype(jnp.bfloat16)
            low_t = (number + 1) % 3
            spots = (
                (
                    (jnp.where(is_z, 1, low_t), jnp.where(is_z, 2, 1)),
                    (jnp.where(is_z, 1, low_t + 1), jnp.where(is_z, 3, 1)),
                    jnp.where(is_z, 1, jnp.where(number == 2, 5, number * 2)),
                ),
                (
                    (jnp.where(is_z, 2, low_t), jnp.where(is_z, 0, 2)),
                    (jnp.where(is_z, 2, low_t + 1), jnp.where(is_z, 1, 2)),
                    jnp.where(is_z, 4, jnp.where(number == 2, 6, number * 2 + 1)),
                ),
            )
            kets = (ket_p0, ket_p1)
            for which in range(2):
                low, up, slot = spots[which]
                for lane in range(2):
                    for half in range(2):
                        link_unit(up, slot, mu, lane, half, vall, links, field, kets[which])
                acc_p[number * 2 + which] = link_product(low, sign, vall, kets[which])

        return 0

    lax.fori_loop(0, 4, pair, 0)

    begin = start_ref[0]
    lattice_t = 2 * n_ta

    def inside(t):
        offset = (ta * 2 + t - begin + 2 * lattice_t) % lattice_t
        return jnp.where(offset < TW, 1.0, 0.0)

    before, first_in, last_in, after = (inside(t) for t in (-1, 0, 1, 2))

    def by_part(values, groups):
        rows = []
        for group in range(groups):
            for part in range(2):
                base = group * 32 + part * 8
                rows.append(
                    jnp.concatenate([values[base : base + 8], values[base + 16 : base + 24]], axis=0)
                )
        return jnp.concatenate(rows, axis=1)

    spaces = [by_part(acc_s[t], 1) for t in range(2)]
    times_in, times_up, times_low = (
        by_part(acc_p[2 * number] + acc_p[2 * number + 1], 2) for number in range(3)
    )
    z_links = [by_part(acc_p[6 + t], 2) for t in range(2)]
    space_in = first_in * spaces[0] + last_in * spaces[1]
    z_in = first_in * z_links[0] + last_in * z_links[1]
    raw = jnp.concatenate(
        [
            jnp.concatenate(
                [spaces[0] + spaces[1], times_in + times_up + times_low, z_links[0] + z_links[1]],
                axis=1,
            ),
            jnp.concatenate(
                [
                    space_in,
                    first_in * times_in + last_in * times_up + before * times_low,
                    z_in,
                ],
                axis=1,
            ),
            jnp.concatenate(
                [
                    space_in,
                    last_in * times_in + after * times_up + first_in * times_low,
                    z_in,
                ],
                axis=1,
            ),
        ],
        axis=0,
    )
    high, rest = split(raw)
    middle, low = split(raw - high.astype(jnp.float32))
    folded = jnp.dot(
        jnp.concatenate([high, middle, low], axis=0),
        table_ref[...],
        preferred_element_type=jnp.float32,
    )
    folded = folded[:48] + folded[48:96] + folded[96:]
    lane = lax.broadcasted_iota(jnp.int32, (1, 128), 1)
    windowed = jnp.where(lane < 64, folded[16:32], folded[32:])
    backward = jnp.transpose(jnp.concatenate([folded[:16], windowed], axis=0))[64:]
    pieces = [
        backward[group * 16 : group * 16 + 16, window * 16 : window * 16 + 16]
        for window in range(2)
        for group in range(4)
    ]
    value = jnp.concatenate([folded[:16, :64], windowed[:, :64]], axis=1)
    value = value + jnp.concatenate(pieces, axis=1)

    if comm:
        for number, (group, index) in enumerate(stages):
            slots[number, index] = value
            copies = []
            for hop in (4, 3, 5, 2, 6, 1, 7):
                copy = pltpu.make_async_remote_copy(
                    src_ref=slots.at[number, index],
                    dst_ref=slots.at[number, index],
                    send_sem=sum_send.at[number, hop],
                    recv_sem=sum_recv.at[number, index],
                    device_id=group((index + hop) % 8),
                    device_id_type=MESH,
                )
                copy.start()
                copies.append(copy)
            for hop in range(1, 8):
                peer = (index + hop) % 8
                pltpu.make_async_remote_copy(
                    src_ref=slots.at[number, peer],
                    dst_ref=slots.at[number, peer],
                    send_sem=sum_send.at[number, hop],
                    recv_sem=sum_recv.at[number, peer],
                    device_id=group(peer),
                    device_id_type=MESH,
                ).wait_recv()
            value = slots[number, 0]
            for other in range(1, 8):
                value = value + slots[number, other]
            for copy in copies:
                copy.wait_send()
        for item in (down_z, up_z, *down_t, *up_t, edge_z, edge_t):
            guarded(item[1], item[0].wait_send)

    charge = jnp.zeros((1, 128), jnp.float32)
    for mode in range(MODES):
        charge = jnp.where(lane % 16 == mode, charge_ref[mode].astype(jnp.float32), charge)
    charge = charge / 3.0
    volume = 24.0 * SITES * (2 * n_gz)
    scale = jnp.where(
        lane < 64, 1.0 / math.sqrt(volume * lattice_t), 1.0 / math.sqrt(volume * TW)
    )
    scale = scale * jnp.where(lane // 16 % 2 == 0, charge, charge * charge)
    out_ref[...] = value * scale


def insert_sums(counts, comm, low, links, photon, charges, start):
    vmem = pl.BlockSpec(memory_space=pltpu.VMEM)
    smem = pl.BlockSpec(memory_space=pltpu.SMEM)
    return pl.pallas_call(
        functools.partial(hop_kernel, counts, comm),
        out_shape=jax.ShapeDtypeStruct((MODES, 128), jnp.float32),
        in_specs=[smem, smem, pl.BlockSpec(memory_space=pl.ANY), vmem, vmem, vmem],
        out_specs=vmem,
        scratch_shapes=[
            pltpu.VMEM((4, 4, SC, 32, SITES), jnp.bfloat16),
            pltpu.VMEM((ROWS, 2 * SITES), jnp.float32),
            pltpu.VMEM((ROWS, 2 * SITES), jnp.float32),
            pltpu.VMEM((SITES, 2 * SITES), jnp.bfloat16),
            pltpu.VMEM((7, 72, 8, SITES), jnp.float32),
            pltpu.VMEM((7, 4, 8, SITES), jnp.float32),
            pltpu.VMEM((3, EDGE, SITES), jnp.float32),
            pltpu.VMEM((3, EDGE, SITES), jnp.float32),
            pltpu.VMEM((256, SC * 128), jnp.bfloat16),
            pltpu.VMEM((256, SC * 128), jnp.bfloat16),
            pltpu.VMEM((128, SC * SITES), jnp.bfloat16),
            pltpu.VMEM((128, SC * SITES), jnp.bfloat16),
            pltpu.VMEM((2, 32, 256), jnp.float32),
            pltpu.VMEM((8, 64, 128), jnp.float32),
            pltpu.VMEM((3, 8, MODES, 128), jnp.float32),
            pltpu.SemaphoreType.DMA((4,)),
            pltpu.SemaphoreType.DMA((8,)),
            pltpu.SemaphoreType.DMA((8,)),
            pltpu.SemaphoreType.DMA((3, 8)),
            pltpu.SemaphoreType.DMA((3, 8)),
        ],
        compiler_params=pltpu.CompilerParams(
            collective_id=0 if comm else None,
            has_side_effects=comm,
            vmem_limit_bytes=40 * 1024 * 1024,
        ),
    )(start, charges, low, links, photon, jnp.asarray(fold_table(), jnp.bfloat16))


def per_device(counts, comm, low_modes, gauge_links, photon, charges, window_start):
    low = low_modes.reshape(2, 8, 2, SC, 2, 2, SITES)
    low = low.transpose(4, 5, 3, 0, 2, 1, 6).reshape(2, 2, SC, 32, SITES)
    sums = insert_sums(counts, comm, low, gauge_links, photon, charges, window_start)
    sums = sums.reshape(MODES, 2, 2, 2, MODES)
    return tuple(
        jnp.transpose(sums[:, window, :, order], (1, 0, 2))
        for window in range(2)
        for order in range(2)
    )


def solution(mesh):
    counts = (mesh.shape["gz"], mesh.shape["ta"])
    return jax.shard_map(
        functools.partial(per_device, counts, True),
        mesh=mesh,
        in_specs=(
            P(None, None, None, None, "ta", "gz", None),
            P(None, None, "ta", "gz", None),
            P(None, "ta", "gz", None),
            P(),
            P(),
        ),
        out_specs=(P(), P(), P(), P()),
        check_vma=False,
    )
```

time: 62.7 us -> 48 us (0.77)
  the two profiles are of different devices: /device:TPU:1 before, /device:TPU:2 now
where the time goes in v2:
time: 48 us; the launch traced here: 47.8 us
  Pallas kernels  42.8 us (89%)
  local copies, waits for them, and re-layouts  3.68 us (8%)
  between operations  1.36 us (3%)
    pallas_call x1, Pallas kernels, insert_sums(): pl.pallas_call(functools.partial(hop_kernel, counts, comm), out_shape=jax...  42.8 us
    reshape x1, local copies, waits for them, and re-layouts, per_device(): low = low_modes.reshape(2, 8, 2, SC, 2, 2, SITES)  1.63 us
    transpose x2, local copies, waits for them, and re-layouts, per_device(): jnp.transpose(sums[:, window, :, order], (1, 0, 2))  1.23 us

profile of v2, /device:TPU:2, one launch (start us, length us, event | category | flops | bytes accessed | tf_op | source)
XLA Modules:
  0.0 47.8 jit_solution(4061397334369755226)
XLA Ops:
  1.3 0.0 copy-start
  1.3 0.0 copy-start.1
  1.3 0.0 copy-start.2
  1.3 1.6 %copy.10 = bf16[2,8,2,12,2,2,256]{6,1,2,0,3,5,4:T(8,128)(2,1)S(1)} copy(bf16[2,8,2,12,2,2,256]{6,5,4,3,2,1,0:T(2,128)(2,1)} %bitcast.21) | data formatting | bytes 1572864 | tf_op jit(solution)/shard_map/reshape | solution.py:618
  2.9 0.0 copy-start.3
  3.0 0.0 copy-done
  3.0 0.0 copy-done.1
  3.0 0.0 copy-done.2
  3.0 0.6 %copy-done.3 = s32[16]{0:T(128)S(1)} copy-done((s32[16]{0:T(128)S(1)}, s32[16]{0:T(128)}, u32[]{:S(2)}) %copy-start.3) | copy-done | bytes 88
  3.6 42.8 %shard_map.93 = f32[16,128]{1,0:T(8,128)S(1)} custom-call(s32[1]{0:T(128)S(6)} %copy.23.start_ref, s32[16]{0:T(128)S(1)} %copy-done.3, bf16[2,2,12,32,256]{4,3,2,1,0:T(8,128)(2,1)S(1)} %bitcast.20, f32[4,18,2,2,256]{4,3,2,1,0:T(2,128)S(1)} %copy-done.1, f32[4,2,2,256]{3,2,1,0:T(2,128)S(1)} %copy-done.2, bf16[1536,128]{1,0:T(8,128)(2,1)S(1)} %copy-done), custom_call_target="tpu_custom_call" | custom-call | tf_op jit(solution)/shard_map/pallas_call | solution.py:582
  46.4 0.1 reshape.19
  46.5 0.1 fusion
  46.6 0.6 %copy_bitcast_fusion = (f32[2,16,16]{2,1,0:T(8,128)}, f32[2,16,16]{2,1,0:T(8,128)}) fusion(f32[16,1,2,1,16]{4,3,2,1,0:T(1,128)S(1)} %get-tuple-element.4, f32[16,1,2,1,16]{4,3,2,1,0:T(1,128)S(1)} %get-tuple-element.5), kind=kLoop, calls=%fused_computation | loop fusion | bytes 8192 | tf_op jit(solution)/shard_map/transpose | solution.py:623
  47.2 0.6 %copy_bitcast_fusion.2 = (f32[2,16,16]{2,1,0:T(8,128)}, f32[2,16,16]{2,1,0:T(8,128)}) fusion(f32[16,1,2,1,16]{4,3,2,1,0:T(1,128)S(1)} %get-tuple-element.6, f32[16,1,2,1,16]{4,3,2,1,0:T(1,128)S(1)} %get-tuple-element.7), kind=kLoop, calls=%fused_computation.2 | loop fusion | bytes 8192 | tf_op jit(solution)/shard_map/transpose | solution.py:623
Async XLA Ops:
  1.3 1.7 %copy-start = (bf16[1536,128]{1,0:T(8,128)(2,1)S(1)}, bf16[1536,128]{1,0:T(8,128)(2,1)}, u32[]{:S(2)}) copy-start(bf16[1536,128]{1,0:T(8,128)(2,1)} %constant.2.clone.table_ref) | copy-start | bytes 1179652
  1.3 1.7 %copy-start.1 = (f32[4,18,2,2,256]{4,3,2,1,0:T(2,128)S(1)}, f32[4,18,2,2,256]{4,3,2,1,0:T(2,128)}, u32[]{:S(2)}) copy-start(f32[4,18,2,2,256]{4,3,2,1,0:T(2,128)} %link_ref.1) | copy-start | bytes 884740
  1.3 1.7 %copy-start.2 = (f32[4,2,2,256]{3,2,1,0:T(2,128)S(1)}, f32[4,2,2,256]{3,2,1,0:T(2,128)}, u32[]{:S(2)}) copy-start(f32[4,2,2,256]{3,2,1,0:T(2,128)} %photon_ref.1) | copy-start | bytes 49156
  2.9 0.7 %copy-start.3 = (s32[16]{0:T(128)S(1)}, s32[16]{0:T(128)}, u32[]{:S(2)}) copy-start(s32[16]{0:T(128)} %charge_ref.1) | copy-start | bytes 196

commit v3 on v2

--- a/solution.py
+++ b/solution.py
@@ -146,12 +146,19 @@
                 store_pair(ket, half * 128 + kind * 32, (spin * 3 + a) * 128, sums[kind][spin])
 
 
-def space_product(t, zz, lane, vall, ket):
+def space_product(t, zz, lane, chunk, vall, ket):
     lanes = slice(lane * 128, lane * 128 + 128)
-    bra = jnp.concatenate([vall[t + 1, zz + 1, sc, :, lanes] for sc in range(SC)], axis=1)
-    return lax.dot_general(
-        bra, ket[...], (((1,), (1,)), ((), ())), preferred_element_type=jnp.float32
-    )
+    scs = range(chunk * 6, chunk * 6 + 6)
+    bra = jnp.concatenate([vall[t + 1, zz + 1, sc, :, lanes] for sc in scs], axis=1)
+    return [
+        lax.dot_general(
+            bra,
+            ket[half * 128 : half * 128 + 128, chunk * 768 : chunk * 768 + 768],
+            (((1,), (1,)), ((), ())),
+            preferred_element_type=jnp.float32,
+        )
+        for half in range(2)
+    ]
 
 
 def link_unit(up, slot, mu, lane, half, vall, links, field, ket):
@@ -170,28 +177,48 @@
             store_pair(ket, half * 64 + 32, column, (photon * re, photon * im))
 
 
-def link_product(low, sign, vall, ket):
-    pieces = [vall[low[0], low[1], sc] for sc in range(SC)]
-    turned = [pieces[(sc + 6) % SC] for sc in range(SC)]
-    turned = [piece * sign if sc // 3 in (0, 3) else piece for sc, piece in enumerate(turned)]
+def link_product(low, sign, chunk, vall, ket):
+    scs = range(chunk * 3, chunk * 3 + 3)
+    pieces = [vall[low[0], low[1], sc] for sc in scs]
+    turned = [vall[low[0], low[1], (sc + 6) % SC] for sc in scs]
+    if chunk in (0, 3):
+        turned = [piece * sign for piece in turned]
     bra = jnp.concatenate(
         [jnp.concatenate(pieces, axis=1), jnp.concatenate(turned, axis=1)], axis=0
     )
-    return lax.dot_general(
-        bra, ket[...], (((1,), (1,)), ((), ())), preferred_element_type=jnp.float32
-    )
+    return [
+        lax.dot_general(
+            bra,
+            ket[half * 64 : half * 64 + 64, chunk * 768 : chunk * 768 + 768],
+            (((1,), (1,)), ((), ())),
+            preferred_element_type=jnp.float32,
+        )
+        for half in range(2)
+    ]
+
+
+def plus(totals, parts):
+    if totals is None:
+        return parts
+    return [total + part for total, part in zip(totals, parts)]
 
 
 def hop_kernel(
     counts,
     comm,
-    start_ref,
-    charge_ref,
+    start_hbm,
+    charge_hbm,
     low_ref,
     link_ref,
     photon_ref,
     table_ref,
     out_ref,
+    start_ref,
+    charge_ref,
+    raw,
+    raw_links,
+    raw_photon,
+    table,
     vall,
     vxy_a,
     vxy_b,
@@ -206,7 +233,9 @@
     ket_p1,
     acc_s,
     acc_p,
+    share,
     slots,
+    whole,
     local_sem,
     send_sem,
     recv_sem,
@@ -214,6 +243,22 @@
     sum_recv,
 ):
     n_gz, n_ta = counts
+    own = [
+        pltpu.make_async_copy(src, dst, local_sem.at[number])
+        for number, (src, dst) in enumerate(
+            (
+                (low_ref, raw),
+                (link_ref, raw_links),
+                (photon_ref, raw_photon),
+                (table_ref, table),
+                (start_hbm, start_ref),
+                (charge_hbm, charge_ref),
+            )
+        )
+    ]
+    for copy in own:
+        copy.start()
+
     if comm:
         gz, ta = lax.axis_index("gz"), lax.axis_index("ta")
     else:
@@ -222,24 +267,39 @@
     def at(g, t):
         return {"gz": g, "ta": t}
 
-    z_hi, x = gz // 4, gz % 4
-    y, z_lo, core = ta // 4, (ta // 2) % 2, ta % 2
+    def wrapped(value, count):
+        return jnp.where(value >= count, value - count, value)
+
+    z_hi = lax.div(gz, 4)
+    x = gz - z_hi * 4
+    y = lax.div(ta, 4)
+    inner = ta - y * 4
+    z_lo = lax.div(inner, 2)
+    core = inner - z_lo * 2
     z = z_hi * 2 + z_lo
 
-    def group_a(index):
-        return at(z_hi * 4 + index // 2, y * 4 + z_lo * 2 + index % 2)
-
-    def group_b(index):
-        return at((index // 2) * 4 + x, y * 4 + (index % 2) * 2 + core)
-
-    def group_c(index):
-        return at(gz, index * 4 + z_lo * 2 + core)
-
-    stages = ((group_a, x * 2 + core), (group_b, z), (group_c, y))
-    below_z = at((gz + n_gz - 1) % n_gz, ta)
-    above_z = at((gz + 1) % n_gz, ta)
-    below_t = at(gz, (ta + n_ta - 1) % n_ta)
-    above_t = at(gz, (ta + 1) % n_ta)
+    others_x, others_z, others_y = [], [], []
+    for dx in (2, 1, 3):
+        peer_x = wrapped(x + dx, 4)
+        others_x.append((peer_x, at(z_hi * 4 + peer_x, ta)))
+    for dz in (2, 1, 3, 0):
+        peer_hi = wrapped(z_hi + dz, 4) if dz else z_hi
+        for peer_lo in (z_lo, 1 - z_lo):
+            if dz or peer_lo is not z_lo:
+                others_z.append(
+                    (peer_hi * 2 + peer_lo, at(peer_hi * 4 + x, ta + (peer_lo - z_lo) * 2))
+                )
+    for dy in (4, 3, 5, 2, 6, 1, 7):
+        peer_y = wrapped(y + dy, 8)
+        others_y.append((peer_y, at(gz, peer_y * 4 + inner)))
+    stages = ((others_x, x), (others_z, z), (others_y, y))
+    partner = at(gz, ta + 1 - 2 * core)
+    is_first, is_second = core == 0, core == 1
+
+    below_z = at(jnp.where(gz == 0, n_gz - 1, gz - 1), ta)
+    above_z = at(wrapped(gz + 1, n_gz), ta)
+    below_t = at(gz, jnp.where(ta == 0, n_ta - 1, ta - 1))
+    above_t = at(gz, wrapped(ta + 1, n_ta))
 
     first_kind = z_lo == 0
     upper_up = jnp.logical_and(
@@ -262,23 +322,14 @@
 
     barrier = pltpu.get_barrier_semaphore() if comm else None
     if comm:
-        for device in (below_z, above_z, below_t, above_t):
+        for device in (below_z, above_z, below_t, above_t, partner):
             pl.semaphore_signal(barrier, inc=1, device_id=device, device_id_type=MESH)
-        for group, index in stages:
-            for step in range(1, 8):
-                pl.semaphore_signal(
-                    barrier, inc=1, device_id=group((index + step) % 8), device_id_type=MESH
-                )
-
-    own = [
-        pltpu.make_async_copy(
-            low_ref.at[t, zz], vall.at[t + 1, zz + 1], local_sem.at[t * 2 + zz]
-        )
-        for t in range(2)
-        for zz in range(2)
-    ]
-    for copy in own:
-        copy.start()
+
+        @pl.when(is_second)
+        def _():
+            for group, _ in stages:
+                for _, device in group:
+                    pl.semaphore_signal(barrier, inc=1, device_id=device, device_id_type=MESH)
 
     def copy_to(src, dst, which, device):
         if comm:
@@ -292,14 +343,14 @@
             )
         return pltpu.make_async_copy(src, dst, recv_sem.at[which])
 
-    down_z = (copy_to(low_ref.at[0, 0], vall.at[1, 3], 0, below_z), always, always)
-    up_z = (copy_to(low_ref.at[1, 1], vall.at[2, 0], 1, above_z), always, always)
+    down_z = (copy_to(vall.at[1, 1], vall.at[1, 3], 0, below_z), always, always)
+    up_z = (copy_to(vall.at[2, 2], vall.at[2, 0], 1, above_z), always, always)
     down_t = [
-        (copy_to(low_ref.at[0, zz], vall.at[3, zz + 1], 2 + zz, below_t), lower_down, upper_down)
+        (copy_to(vall.at[1, zz + 1], vall.at[3, zz + 1], 2 + zz, below_t), lower_down, upper_down)
         for zz in range(2)
     ]
     up_t = [
-        (copy_to(low_ref.at[1, zz], vall.at[0, zz + 1], 4 + zz, above_t), upper_up, lower_up)
+        (copy_to(vall.at[2, zz + 1], vall.at[0, zz + 1], 4 + zz, above_t), upper_up, lower_up)
         for zz in range(2)
     ]
     edge_z = (copy_to(edge_out.at[0], edge_in.at[0], 6, above_z), always, always)
@@ -321,20 +372,57 @@
     def arrive(item):
         guarded(item[2], item[0].wait_recv if comm else item[0].wait)
 
+    row = lax.broadcasted_iota(jnp.int32, (SITES, SITES), 0)
+    column = lax.broadcasted_iota(jnp.int32, (SITES, SITES), 1)
+    along_x = (column + LY) % SITES
+    along_y = (column - column % LY) + (column + 1) % LY
+    perm[:, :SITES] = (row == along_x).astype(jnp.float32).astype(jnp.bfloat16)
+    perm[:, SITES:] = (row == along_y).astype(jnp.float32).astype(jnp.bfloat16)
+    acc_s[...] = jnp.zeros_like(acc_s)
+    acc_p[...] = jnp.zeros_like(acc_p)
+    ket_s1[...] = jnp.zeros_like(ket_s1)
+    ket_p1[...] = jnp.zeros_like(ket_p1)
+
+    def arrange(t):
+        def one_spin(spin, _):
+            for colour in range(3):
+                parts = [
+                    jnp.swapaxes(raw[:, part, spin, colour, t].astype(jnp.float32), 0, 1)
+                    for part in range(2)
+                ]
+                for zz in range(2):
+                    for half in range(2):
+                        vall[
+                            t + 1, zz + 1, spin * 3 + colour, half * 16 : half * 16 + 16, :
+                        ] = jnp.concatenate(
+                            [part[zz, half * 8 : half * 8 + 8] for part in parts], axis=0
+                        ).astype(jnp.bfloat16)
+            return 0
+
+        lax.fori_loop(0, 4, one_spin, 0)
+
+    own[0].wait()
+    arrange(0)
     if comm:
-        pl.semaphore_wait(barrier, 25)
-    for item in (down_z, up_z, *down_t, *up_t):
+        pl.semaphore_wait(barrier, jnp.where(is_second, 22, 5))
+    for item in (down_z, *down_t):
         start(item)
+    arrange(1)
+    for item in (up_z, *up_t):
+        start(item)
+
+    own[1].wait()
+    own[2].wait()
 
     def spread(t, _):
         turn = jnp.where(jnp.logical_and(ta == n_ta - 1, t == 1), -1.0, 1.0)
         for mu in range(4):
-            photon = photon_ref[mu, t]
+            photon = raw_photon[mu, t]
             scale = photon * turn if mu == 3 else photon
             for zz in range(2):
                 field[t * 2 + zz, mu] = jnp.broadcast_to(photon[zz : zz + 1], (8, SITES))
             for entry in range(18):
-                scaled = link_ref[mu, entry, t] * scale
+                scaled = raw_links[mu, entry, t] * scale
                 for zz in range(2):
                     links[t * 2 + zz, mu * 18 + entry] = jnp.broadcast_to(
                         scaled[zz : zz + 1], (8, SITES)
@@ -351,17 +439,6 @@
     start(edge_z)
     start(edge_t)
 
-    row = lax.broadcasted_iota(jnp.int32, (SITES, SITES), 0)
-    column = lax.broadcasted_iota(jnp.int32, (SITES, SITES), 1)
-    along_x = (column + LY) % SITES
-    along_y = (column - column % LY) + (column + 1) % LY
-    perm[:, :SITES] = (row == along_x).astype(jnp.float32).astype(jnp.bfloat16)
-    perm[:, SITES:] = (row == along_y).astype(jnp.float32).astype(jnp.bfloat16)
-
-    acc_p[...] = jnp.zeros_like(acc_p)
-    for copy in own:
-        copy.wait()
-
     def shift(t, zz, vxy):
         vxy[...] = jnp.dot(
             vall[t + 1, zz + 1].reshape(ROWS, SITES),
@@ -373,24 +450,27 @@
 
     def blocks(t, _):
         kets = (ket_s0, ket_s1)
-        total = None
-        pending = None
+        before = jnp.maximum(t - 1, 0)
+        pending = (before, 1, 1)
         for zz, vxy in ((0, vxy_a), (1, vxy_b)):
-            if zz == 0:
-                shift(t, 1, vxy_b)
             for lane in range(2):
-                if pending is not None:
-                    product = space_product(t, *pending, vall, kets[pending[1]])
-                    total = product if total is None else total + product
+                if zz == 0 and lane == 0:
+                    shift(t, 1, vxy_b)
+                totals = None
                 for half in range(2):
                     space_unit(t, zz, lane, half, vall, vxy, links, field, kets[lane])
-                pending = (zz, lane)
-            if zz == 0:
-                shift(jnp.minimum(t + 1, 1), 0, vxy_a)
-        acc_s[t] = total + space_product(t, *pending, vall, kets[pending[1]])
+                    totals = plus(totals, space_product(*pending, half, vall, kets[pending[2]]))
+                for half in range(2):
+                    acc_s[pending[0], half] += totals[half]
+                pending = (t, zz, lane)
+                if zz == 1 and lane == 0:
+                    shift(jnp.minimum(t + 1, 1), 0, vxy_a)
         return 0
 
     lax.fori_loop(0, 2, blocks, 0)
+    for chunk in range(2):
+        for half, part in enumerate(space_product(1, 1, 1, chunk, vall, ket_s1)):
+            acc_s[1, half] += part
 
     def spread_edge(number, slot, mu):
         for entry in range(18):
@@ -399,32 +479,33 @@
             )
         field[slot, mu] = jnp.broadcast_to(edge_in[number, 18:19], (8, SITES))
 
-    def pair(number, _):
+    z_first = jnp.where(x == 0, 0, 1)
+
+    def place(number, which):
+        z_t = z_first if which == 0 else 1 - z_first
         is_z = number == 3
-
-        @pl.when(number == 1)
-        def _():
-            arrive(down_t[0])
-            arrive(down_t[1])
-
-        @pl.when(number == 2)
-        def _():
-            arrive(up_t[0])
-            arrive(up_t[1])
-            arrive(edge_t)
-
-            @pl.when(lower_up)
-            def _():
-                spread_edge(1, 5, 3)
-                spread_edge(2, 6, 3)
-
-        @pl.when(is_z)
-        def _():
-            arrive(down_z)
-            arrive(up_z)
-            arrive(edge_z)
-            spread_edge(0, 4, 2)
-
+        low_t = lax.rem(number + 1, 3)
+        low = (jnp.where(is_z, z_t + 1, low_t), jnp.where(is_z, 2 - 2 * z_t, which + 1))
+        up = (jnp.where(is_z, z_t + 1, low_t + 1), jnp.where(is_z, 3 - 2 * z_t, which + 1))
+        slot = jnp.where(
+            is_z, 1 + 3 * z_t, jnp.where(number == 2, 5, number * 2) + which
+        )
+        product = number * 2 + jnp.where(is_z, z_t, which)
+        sign = jnp.where(is_z, -1.0, 1.0).astype(jnp.bfloat16)
+        return low, up, slot, product, sign, z_t
+
+    def product_of(number, which, ket, units=None):
+        low, _, _, product, sign, _ = place(number, which)
+        totals = None
+        for chunk in range(4):
+            if units is not None:
+                units(chunk)
+            totals = plus(totals, link_product(low, sign, chunk, vall, ket))
+        for half in range(2):
+            acc_p[product, half] = totals[half]
+
+    def pair(number, previous):
+        is_z = number == 3
         active = jnp.logical_or(
             jnp.logical_or(number == 0, is_z),
             jnp.logical_or(
@@ -434,33 +515,49 @@
 
         @pl.when(active)
         def _():
-            mu = jnp.where(is_z, 2, 3)
-            sign = jnp.where(is_z, -1.0, 1.0).astype(jnp.bfloat16)
-            low_t = (number + 1) % 3
-            spots = (
-                (
-                    (jnp.where(is_z, 1, low_t), jnp.where(is_z, 2, 1)),
-                    (jnp.where(is_z, 1, low_t + 1), jnp.where(is_z, 3, 1)),
-                    jnp.where(is_z, 1, jnp.where(number == 2, 5, number * 2)),
-                ),
-                (
-                    (jnp.where(is_z, 2, low_t), jnp.where(is_z, 0, 2)),
-                    (jnp.where(is_z, 2, low_t + 1), jnp.where(is_z, 1, 2)),
-                    jnp.where(is_z, 4, jnp.where(number == 2, 6, number * 2 + 1)),
-                ),
-            )
-            kets = (ket_p0, ket_p1)
-            for which in range(2):
-                low, up, slot = spots[which]
-                for lane in range(2):
-                    for half in range(2):
-                        link_unit(up, slot, mu, lane, half, vall, links, field, kets[which])
-                acc_p[number * 2 + which] = link_product(low, sign, vall, kets[which])
-
-        return 0
-
-    lax.fori_loop(0, 4, pair, 0)
-
+            for which, ket in enumerate((ket_p0, ket_p1)):
+                _, up, slot, _, _, z_t = place(number, which)
+
+                @pl.when(number == 1)
+                def _():
+                    arrive(down_t[which])
+
+                @pl.when(number == 2)
+                def _():
+                    arrive(up_t[which])
+                    if which == 0:
+                        arrive(edge_t)
+
+                    @pl.when(lower_up)
+                    def _():
+                        spread_edge(1 + which, 5 + which, 3)
+
+                @pl.when(jnp.logical_and(is_z, z_t == 0))
+                def _():
+                    arrive(down_z)
+
+                @pl.when(jnp.logical_and(is_z, z_t == 1))
+                def _():
+                    arrive(up_z)
+                    arrive(edge_z)
+                    spread_edge(0, 4, 2)
+
+                mu = jnp.where(is_z, 2, 3)
+
+                def units(step, up=up, slot=slot, ket=ket):
+                    link_unit(up, slot, mu, step // 2, step % 2, vall, links, field, ket)
+
+                if which == 0:
+                    product_of(previous, 1, ket_p1, units)
+                else:
+                    product_of(number, 0, ket_p0, units)
+
+        return jnp.where(active, number, previous)
+
+    lax.fori_loop(0, 4, pair, jnp.int32(0))
+    product_of(jnp.int32(3), 1, ket_p1)
+
+    own[4].wait()
     begin = start_ref[0]
     lattice_t = 2 * n_ta
 
@@ -480,14 +577,17 @@
                 )
         return jnp.concatenate(rows, axis=1)
 
-    spaces = [by_part(acc_s[t], 1) for t in range(2)]
+    def both(acc, index):
+        return jnp.concatenate([acc[index, 0], acc[index, 1]], axis=1)
+
+    spaces = [by_part(both(acc_s, t), 1) for t in range(2)]
     times_in, times_up, times_low = (
-        by_part(acc_p[2 * number] + acc_p[2 * number + 1], 2) for number in range(3)
-    )
-    z_links = [by_part(acc_p[6 + t], 2) for t in range(2)]
+        by_part(both(acc_p, 2 * number) + both(acc_p, 2 * number + 1), 2) for number in range(3)
+    )
+    z_links = [by_part(both(acc_p, 6 + t), 2) for t in range(2)]
     space_in = first_in * spaces[0] + last_in * spaces[1]
     z_in = first_in * z_links[0] + last_in * z_links[1]
-    raw = jnp.concatenate(
+    products = jnp.concatenate(
         [
             jnp.concatenate(
                 [spaces[0] + spaces[1], times_in + times_up + times_low, z_links[0] + z_links[1]],
@@ -512,11 +612,13 @@
         ],
         axis=0,
     )
-    high, rest = split(raw)
-    middle, low = split(raw - high.astype(jnp.float32))
+    own[3].wait()
+    own[5].wait()
+    high, rest = split(products)
+    middle, low = split(products - high.astype(jnp.float32))
     folded = jnp.dot(
         jnp.concatenate([high, middle, low], axis=0),
-        table_ref[...],
+        table[...],
         preferred_element_type=jnp.float32,
     )
     folded = folded[:48] + folded[48:96] + folded[96:]
@@ -532,35 +634,64 @@
     value = value + jnp.concatenate(pieces, axis=1)
 
     if comm:
-        for number, (group, index) in enumerate(stages):
-            slots[number, index] = value
-            copies = []
-            for hop in (4, 3, 5, 2, 6, 1, 7):
-                copy = pltpu.make_async_remote_copy(
-                    src_ref=slots.at[number, index],
-                    dst_ref=slots.at[number, index],
-                    send_sem=sum_send.at[number, hop],
-                    recv_sem=sum_recv.at[number, index],
-                    device_id=group((index + hop) % 8),
-                    device_id_type=MESH,
-                )
-                copy.start()
-                copies.append(copy)
-            for hop in range(1, 8):
-                peer = (index + hop) % 8
-                pltpu.make_async_remote_copy(
-                    src_ref=slots.at[number, peer],
-                    dst_ref=slots.at[number, peer],
-                    send_sem=sum_send.at[number, hop],
-                    recv_sem=sum_recv.at[number, peer],
-                    device_id=group(peer),
-                    device_id_type=MESH,
-                ).wait_recv()
-            value = slots[number, 0]
-            for other in range(1, 8):
-                value = value + slots[number, other]
-            for copy in copies:
+
+        def to_partner(ref, number):
+            return pltpu.make_async_remote_copy(
+                src_ref=ref,
+                dst_ref=ref,
+                send_sem=sum_send.at[number, 7],
+                recv_sem=sum_recv.at[3, number],
+                device_id=partner,
+                device_id_type=MESH,
+            )
+
+        hand_over = to_partner(share, 0)
+        hand_back = to_partner(whole, 1)
+
+        @pl.when(is_first)
+        def _():
+            share[...] = value
+            hand_over.start()
+            hand_back.wait_recv()
+            hand_over.wait_send()
+
+        @pl.when(is_second)
+        def _():
+            hand_over.wait_recv()
+            total = value + share[...]
+            started = []
+            for number, (others, index) in enumerate(stages):
+                slots[number, index] = total
+                for step, (_, device) in enumerate(others):
+                    copy = pltpu.make_async_remote_copy(
+                        src_ref=slots.at[number, index],
+                        dst_ref=slots.at[number, index],
+                        send_sem=sum_send.at[number, step],
+                        recv_sem=sum_recv.at[number, index],
+                        device_id=device,
+                        device_id_type=MESH,
+                    )
+                    copy.start()
+                    started.append(copy)
+                for step, (peer, device) in enumerate(others):
+                    pltpu.make_async_remote_copy(
+                        src_ref=slots.at[number, peer],
+                        dst_ref=slots.at[number, peer],
+                        send_sem=sum_send.at[number, step],
+                        recv_sem=sum_recv.at[number, peer],
+                        device_id=device,
+                        device_id_type=MESH,
+                    ).wait_recv()
+                total = slots[number, 0]
+                for other in range(1, len(others) + 1):
+                    total = total + slots[number, other]
+            whole[...] = total
+            hand_back.start()
+            for copy in started:
                 copy.wait_send()
+            hand_back.wait_send()
+
+        value = whole[...]
         for item in (down_z, up_z, *down_t, *up_t, edge_z, edge_t):
             guarded(item[1], item[0].wait_send)
 
@@ -578,13 +709,18 @@
 
 def insert_sums(counts, comm, low, links, photon, charges, start):
     vmem = pl.BlockSpec(memory_space=pltpu.VMEM)
-    smem = pl.BlockSpec(memory_space=pltpu.SMEM)
     return pl.pallas_call(
         functools.partial(hop_kernel, counts, comm),
         out_shape=jax.ShapeDtypeStruct((MODES, 128), jnp.float32),
-        in_specs=[smem, smem, pl.BlockSpec(memory_space=pl.ANY), vmem, vmem, vmem],
+        in_specs=[pl.BlockSpec(memory_space=pl.ANY)] * 6,
         out_specs=vmem,
         scratch_shapes=[
+            pltpu.SMEM(start.shape, start.dtype),
+            pltpu.SMEM(charges.shape, charges.dtype),
+            pltpu.VMEM(low.shape, low.dtype),
+            pltpu.VMEM(links.shape, links.dtype),
+            pltpu.VMEM(photon.shape, photon.dtype),
+            pltpu.VMEM((1536, 128), jnp.bfloat16),
             pltpu.VMEM((4, 4, SC, 32, SITES), jnp.bfloat16),
             pltpu.VMEM((ROWS, 2 * SITES), jnp.float32),
             pltpu.VMEM((ROWS, 2 * SITES), jnp.float32),
@@ -597,27 +733,27 @@
             pltpu.VMEM((256, SC * 128), jnp.bfloat16),
             pltpu.VMEM((128, SC * SITES), jnp.bfloat16),
             pltpu.VMEM((128, SC * SITES), jnp.bfloat16),
-            pltpu.VMEM((2, 32, 256), jnp.float32),
-            pltpu.VMEM((8, 64, 128), jnp.float32),
+            pltpu.VMEM((2, 2, 32, 128), jnp.float32),
+            pltpu.VMEM((8, 2, 64, 64), jnp.float32),
+            pltpu.VMEM((MODES, 128), jnp.float32),
             pltpu.VMEM((3, 8, MODES, 128), jnp.float32),
-            pltpu.SemaphoreType.DMA((4,)),
+            pltpu.VMEM((MODES, 128), jnp.float32),
+            pltpu.SemaphoreType.DMA((6,)),
             pltpu.SemaphoreType.DMA((8,)),
             pltpu.SemaphoreType.DMA((8,)),
             pltpu.SemaphoreType.DMA((3, 8)),
-            pltpu.SemaphoreType.DMA((3, 8)),
+            pltpu.SemaphoreType.DMA((4, 8)),
         ],
         compiler_params=pltpu.CompilerParams(
             collective_id=0 if comm else None,
             has_side_effects=comm,
-            vmem_limit_bytes=40 * 1024 * 1024,
+            vmem_limit_bytes=60 * 1024 * 1024,
         ),
     )(start, charges, low, links, photon, jnp.asarray(fold_table(), jnp.bfloat16))
 
 
 def per_device(counts, comm, low_modes, gauge_links, photon, charges, window_start):
-    low = low_modes.reshape(2, 8, 2, SC, 2, 2, SITES)
-    low = low.transpose(4, 5, 3, 0, 2, 1, 6).reshape(2, 2, SC, 32, SITES)
-    sums = insert_sums(counts, comm, low, gauge_links, photon, charges, window_start)
+    sums = insert_sums(counts, comm, low_modes, gauge_links, photon, charges, window_start)
     sums = sums.reshape(MODES, 2, 2, 2, MODES)
     return tuple(
         jnp.transpose(sums[:, window, :, order], (1, 0, 2))

time: 48 us -> 45.3 us (0.944)
  the two profiles are of different devices: /device:TPU:2 before, /device:TPU:1 now
where the time goes in v3:
time: 45.3 us; the launch traced here: 45.1 us
  Pallas kernels  41.7 us (92%)
  local copies, waits for them, and re-layouts  2.11 us (5%)
  between operations  1.3 us (3%)
    pallas_call x1, Pallas kernels, insert_sums(): pl.pallas_call(functools.partial(hop_kernel, counts, comm), out_shape=jax...  41.7 us
    transpose x2, local copies, waits for them, and re-layouts, per_device(): jnp.transpose(sums[:, window, :, order], (1, 0, 2))  1.23 us

profile of v3, /device:TPU:1, one launch (start us, length us, event | category | flops | bytes accessed | tf_op | source)
XLA Modules:
  0.0 45.1 jit_solution(18395973076967079243)
XLA Ops:
  1.3 41.7 %shard_map.93 = f32[16,128]{1,0:T(8,128)} custom-call(s32[1]{0:T(128)S(6)} %copy.22.start_hbm, s32[16]{0:T(128)} %charge_hbm.1, bf16[16,2,4,3,2,2,256]{6,5,4,3,2,1,0:T(2,128)(2,1)} %low_ref.1, f32[4,18,2,2,256]{4,3,2,1,0:T(2,128)} %link_ref.1, f32[4,2,2,256]{3,2,1,0:T(2,128)} %photon_ref.1, bf16[1536,128]{1,0:T(8,128)(2,1)} %constant.2.clone.table_ref), custom_call_target="tpu_custom_call" | custom-call | tf_op jit(solution)/shard_map/pallas_call | solution.py:712
  43.0 0.8 %reshape.11 = f32[16,2,2,2,16]{4,3,2,1,0:T(2,128)S(1)} reshape(f32[16,128]{1,0:T(8,128)} %shard_map.93) | data formatting | bytes 16384 | tf_op jit(solution)/shard_map/reshape | solution.py:757
  43.8 0.1 fusion
  43.9 0.6 %copy_bitcast_fusion = (f32[2,16,16]{2,1,0:T(8,128)}, f32[2,16,16]{2,1,0:T(8,128)}) fusion(f32[16,1,2,1,16]{4,3,2,1,0:T(1,128)S(1)} %get-tuple-element.4, f32[16,1,2,1,16]{4,3,2,1,0:T(1,128)S(1)} %get-tuple-element.5), kind=kLoop, calls=%fused_computation | loop fusion | bytes 8192 | tf_op jit(solution)/shard_map/transpose | solution.py:759
  44.5 0.6 %copy_bitcast_fusion.2 = (f32[2,16,16]{2,1,0:T(8,128)}, f32[2,16,16]{2,1,0:T(8,128)}) fusion(f32[16,1,2,1,16]{4,3,2,1,0:T(1,128)S(1)} %get-tuple-element.6, f32[16,1,2,1,16]{4,3,2,1,0:T(1,128)S(1)} %get-tuple-element.7), kind=kLoop, calls=%fused_computation.2 | loop fusion | bytes 8192 | tf_op jit(solution)/shard_map/transpose | solution.py:759

commit v4 on v3

--- a/solution.py
+++ b/solution.py
@@ -127,23 +127,27 @@
 
     sources = (from_x, from_y, from_z) if zz == 0 else (from_x, from_y)
     for a in range(3):
-        sums = [[[None, None] for _ in range(4)] for _ in range(4)]
-        for mu, source in enumerate(sources):
-            first = colour_row(link_rows(links, slot, mu * 18, a, lanes), source)
-            photon = field[slot, mu, :, lanes]
-            second = [(photon * re, photon * im) for re, im in first]
-            for order, hopped in enumerate((first, second)):
-                for spin in range(4):
-                    plain = sums[order * 2][spin]
-                    crossed = sums[order * 2 + 1][spin]
+        hops = [
+            colour_row(link_rows(links, slot, mu * 18, a, lanes), source)
+            for mu, source in enumerate(sources)
+        ]
+        for order in range(2):
+            if order == 1:
+                for mu in range(len(hops)):
+                    photon = field[slot, mu, :, lanes]
+                    hops[mu] = [(photon * re, photon * im) for re, im in hops[mu]]
+            for spin in range(4):
+                plain = [None, None]
+                crossed = [None, None]
+                for mu, hopped in enumerate(hops):
                     entry = GAMMA[mu][spin]
                     turned = times(entry, hopped[entry[0]])
                     for part in range(2):
                         plain[part] = add_signed(plain[part], 1, hopped[spin][part])
                         crossed[part] = add_signed(crossed[part], *turned[part])
-        for kind in range(4):
-            for spin in range(4):
-                store_pair(ket, half * 128 + kind * 32, (spin * 3 + a) * 128, sums[kind][spin])
+                column = (spin * 3 + a) * 128
+                store_pair(ket, half * 128 + order * 64, column, plain)
+                store_pair(ket, half * 128 + order * 64 + 32, column, crossed)
 
 
 def space_product(t, zz, lane, chunk, vall, ket):
@@ -293,7 +297,16 @@
         peer_y = wrapped(y + dy, 8)
         others_y.append((peer_y, at(gz, peer_y * 4 + inner)))
     stages = ((others_x, x), (others_z, z), (others_y, y))
-    partner = at(gz, ta + 1 - 2 * core)
+    crossed = ta + 1 - 2 * core
+    along_row = [(x, at(gz, crossed))]
+    along_row += [
+        (wrapped(x + dx, 4), at(z_hi * 4 + wrapped(x + dx, 4), crossed)) for dx in (2, 1, 3)
+    ]
+    along_column = [(y, at(gz, crossed))]
+    along_column += [
+        (wrapped(y + dy, 8), at(gz, wrapped(y + dy, 8) * 4 + crossed - y * 4))
+        for dy in (4, 3, 5, 2, 6, 1, 7)
+    ]
     is_first, is_second = core == 0, core == 1
 
     below_z = at(jnp.where(gz == 0, n_gz - 1, gz - 1), ta)
@@ -322,7 +335,9 @@
 
     barrier = pltpu.get_barrier_semaphore() if comm else None
     if comm:
-        for device in (below_z, above_z, below_t, above_t, partner):
+        greeted = [below_z, above_z, below_t, above_t]
+        greeted += [device for _, device in along_row + along_column]
+        for device in greeted:
             pl.semaphore_signal(barrier, inc=1, device_id=device, device_id_type=MESH)
 
         @pl.when(is_second)
@@ -404,7 +419,7 @@
     own[0].wait()
     arrange(0)
     if comm:
-        pl.semaphore_wait(barrier, jnp.where(is_second, 22, 5))
+        pl.semaphore_wait(barrier, jnp.where(is_second, 33, 16))
     for item in (down_z, *down_t):
         start(item)
     arrange(1)
@@ -446,25 +461,35 @@
             preferred_element_type=jnp.float32,
         )
 
+    def shift_half(t, zz, vxy, part):
+        vxy[part * 192 : part * 192 + 192, :] = jnp.dot(
+            vall[t + 1, zz + 1, part * 6 : part * 6 + 6].reshape(192, SITES),
+            perm[...],
+            preferred_element_type=jnp.float32,
+        )
+
     shift(0, 0, vxy_a)
 
     def blocks(t, _):
         kets = (ket_s0, ket_s1)
-        before = jnp.maximum(t - 1, 0)
-        pending = (before, 1, 1)
+        pending = (jnp.maximum(t - 1, 0), 1, 1)
         for zz, vxy in ((0, vxy_a), (1, vxy_b)):
             for lane in range(2):
-                if zz == 0 and lane == 0:
-                    shift(t, 1, vxy_b)
-                totals = None
-                for half in range(2):
-                    space_unit(t, zz, lane, half, vall, vxy, links, field, kets[lane])
-                    totals = plus(totals, space_product(*pending, half, vall, kets[pending[2]]))
-                for half in range(2):
-                    acc_s[pending[0], half] += totals[half]
+
+                @pl.when(core >= 0)
+                def _(zz=zz, vxy=vxy, lane=lane, pending=pending):
+                    totals = None
+                    for half in range(2):
+                        space_unit(t, zz, lane, half, vall, vxy, links, field, kets[lane])
+                        totals = plus(totals, space_product(*pending, half, vall, kets[pending[2]]))
+                    for half in range(2):
+                        acc_s[pending[0], half] += totals[half]
+                    if zz == 0:
+                        shift_half(t, 1, vxy_b, lane)
+                    else:
+                        shift_half(jnp.minimum(t + 1, 1), 0, vxy_a, lane)
+
                 pending = (t, zz, lane)
-                if zz == 1 and lane == 0:
-                    shift(jnp.minimum(t + 1, 1), 0, vxy_a)
         return 0
 
     lax.fori_loop(0, 2, blocks, 0)
@@ -635,61 +660,57 @@
 
     if comm:
 
-        def to_partner(ref, number):
+        def message(src, number, slot, sent, device):
             return pltpu.make_async_remote_copy(
-                src_ref=ref,
-                dst_ref=ref,
-                send_sem=sum_send.at[number, 7],
-                recv_sem=sum_recv.at[3, number],
-                device_id=partner,
+                src_ref=src,
+                dst_ref=slots.at[number, slot],
+                send_sem=sum_send.at[sent],
+                recv_sem=sum_recv.at[number, slot],
+                device_id=device,
                 device_id_type=MESH,
             )
 
-        hand_over = to_partner(share, 0)
-        hand_back = to_partner(whole, 1)
+        def gather(number, found, last):
+            for slot, device in found:
+                message(slots.at[number, slot], number, slot, 0, device).wait_recv()
+            total = slots[number, 0]
+            for other in range(1, last):
+                total = total + slots[number, other]
+            return total
 
         @pl.when(is_first)
         def _():
             share[...] = value
-            hand_over.start()
-            hand_back.wait_recv()
-            hand_over.wait_send()
+            started = [
+                message(share, 0, 4 + x, step, device)
+                for step, (_, device) in enumerate(along_row)
+            ]
+            for copy in started:
+                copy.start()
+            whole[...] = gather(2, along_column, 8)
+            for copy in started:
+                copy.wait_send()
 
         @pl.when(is_second)
         def _():
-            hand_over.wait_recv()
-            total = value + share[...]
+            total = value
             started = []
             for number, (others, index) in enumerate(stages):
                 slots[number, index] = total
-                for step, (_, device) in enumerate(others):
-                    copy = pltpu.make_async_remote_copy(
-                        src_ref=slots.at[number, index],
-                        dst_ref=slots.at[number, index],
-                        send_sem=sum_send.at[number, step],
-                        recv_sem=sum_recv.at[number, index],
-                        device_id=device,
-                        device_id_type=MESH,
-                    )
+                targets = [(index, device) for _, device in others]
+                if number == 2:
+                    targets += [(index, device) for _, device in along_column]
+                for slot, device in targets:
+                    copy = message(slots.at[number, index], number, slot, len(started), device)
                     copy.start()
                     started.append(copy)
-                for step, (peer, device) in enumerate(others):
-                    pltpu.make_async_remote_copy(
-                        src_ref=slots.at[number, peer],
-                        dst_ref=slots.at[number, peer],
-                        send_sem=sum_send.at[number, step],
-                        recv_sem=sum_recv.at[number, peer],
-                        device_id=device,
-                        device_id_type=MESH,
-                    ).wait_recv()
-                total = slots[number, 0]
-                for other in range(1, len(others) + 1):
-                    total = total + slots[number, other]
+                found = list(others)
+                if number == 0:
+                    found += [(4 + place_x, device) for place_x, device in along_row]
+                total = gather(number, found, 8)
             whole[...] = total
-            hand_back.start()
             for copy in started:
                 copy.wait_send()
-            hand_back.wait_send()
 
         value = whole[...]
         for item in (down_z, up_z, *down_t, *up_t, edge_z, edge_t):
@@ -711,7 +732,7 @@
     vmem = pl.BlockSpec(memory_space=pltpu.VMEM)
     return pl.pallas_call(
         functools.partial(hop_kernel, counts, comm),
-        out_shape=jax.ShapeDtypeStruct((MODES, 128), jnp.float32),
+        out_shape=pltpu.VMEM((MODES, 128), jnp.float32),
         in_specs=[pl.BlockSpec(memory_space=pl.ANY)] * 6,
         out_specs=vmem,
         scratch_shapes=[
@@ -741,8 +762,8 @@
             pltpu.SemaphoreType.DMA((6,)),
             pltpu.SemaphoreType.DMA((8,)),
             pltpu.SemaphoreType.DMA((8,)),
+            pltpu.SemaphoreType.DMA((25,)),
             pltpu.SemaphoreType.DMA((3, 8)),
-            pltpu.SemaphoreType.DMA((4, 8)),
         ],
         compiler_params=pltpu.CompilerParams(
             collective_id=0 if comm else None,
@@ -752,14 +773,23 @@
     )(start, charges, low, links, photon, jnp.asarray(fold_table(), jnp.bfloat16))
 
 
+def lay_out(sums, *outputs):
+    for window in range(2):
+        for part in range(2):
+            for order in range(2):
+                start = window * 64 + part * 32 + order * 16
+                outputs[window * 2 + order][part] = sums[:, start : start + 16]
+
+
 def per_device(counts, comm, low_modes, gauge_links, photon, charges, window_start):
     sums = insert_sums(counts, comm, low_modes, gauge_links, photon, charges, window_start)
-    sums = sums.reshape(MODES, 2, 2, 2, MODES)
-    return tuple(
-        jnp.transpose(sums[:, window, :, order], (1, 0, 2))
-        for window in range(2)
-        for order in range(2)
-    )
+    vmem = pl.BlockSpec(memory_space=pltpu.VMEM)
+    return pl.pallas_call(
+        lay_out,
+        out_shape=[jax.ShapeDtypeStruct((2, MODES, MODES), jnp.float32)] * 4,
+        in_specs=[vmem],
+        out_specs=[vmem] * 4,
+    )(sums)
 
 
 def solution(mesh):

time: 45.3 us -> 43.2 us (0.954)
  local copies, waits for them, and re-layouts: 2.11 us -> 0.58 us
  Pallas kernels: 41.7 us -> 41.2 us
    transpose x2 -> x0, local copies, waits for them, and re-layouts: 1.23 us -> none  [per_device(): jnp.transpose(sums[:, window, :, order], (1, 0, 2))]
    reshape x1 -> x0, local copies, waits for them, and re-layouts: 0.83 us -> none  [per_device(): sums = sums.reshape(MODES, 2, 2, 2, MODES)]
    unnamed x0 -> x2, local copies, waits for them, and re-layouts: none -> 0.58 us
    pallas_call x1 -> x2, Pallas kernels: 41.7 us -> 41.2 us  [the longest x1 39.8 us: insert_sums(): pl.pallas_call(functools.partial(hop_kernel, counts, comm), out_shape=plt...]
where the time goes in v4:
time: 43.2 us; the launch traced here: 43 us
  Pallas kernels  41.2 us (95%)
  between operations  1.3 us (3%)
  local copies, waits for them, and re-layouts  0.58 us (1%)
    pallas_call x1, Pallas kernels, insert_sums(): pl.pallas_call(functools.partial(hop_kernel, counts, comm), out_shape=plt...  39.8 us
    pallas_call x1, Pallas kernels, per_device(): pl.pallas_call(lay_out, out_shape=[jax.ShapeDtypeStruct((2, MODES, MODES)...  1.39 us

profile of v4, /device:TPU:1, one launch (start us, length us, event | category | flops | bytes accessed | tf_op | source)
XLA Modules:
  0.0 43.0 jit_solution(5671647535007284866)
XLA Ops:
  1.3 39.8 %shard_map.93.sums = f32[16,128]{1,0:T(8,128)S(1)} custom-call(s32[1]{0:T(128)S(6)} %copy.10.start_hbm, s32[16]{0:T(128)} %charge_hbm.1, bf16[16,2,4,3,2,2,256]{6,5,4,3,2,1,0:T(2,128)(2,1)} %low_ref.1, f32[4,18,2,2,256]{4,3,2,1,0:T(2,128)} %link_ref.1, f32[4,2,2,256]{3,2,1,0:T(2,128)} %photon_ref.1, bf16[1536,128]{1,0:T(8,128)(2,1)} %constant.2.clone.table_ref), custom_call_target="tpu_custom_call" | custom-call | tf_op jit(solution)/shard_map/pallas_call | solution.py:733
  41.1 0.0 copy-start
  41.1 0.6 %copy-done = f32[16,128]{1,0:T(8,128)} copy-done((f32[16,128]{1,0:T(8,128)}, f32[16,128]{1,0:T(8,128)S(1)}, u32[]{:S(2)}) %copy-start) | copy-done | bytes 8216
  41.6 1.4 %shard_map.94 = (f32[2,16,16]{2,1,0:T(8,128)}, f32[2,16,16]{2,1,0:T(8,128)}, f32[2,16,16]{2,1,0:T(8,128)}, f32[2,16,16]{2,1,0:T(8,128)}) custom-call(f32[16,128]{1,0:T(8,128)} %copy-done), custom_call_target="tpu_custom_call" | custom-call | tf_op jit(solution)/shard_map/pallas_call | solution.py:787
Async XLA Ops:
  41.1 0.6 %copy-start = (f32[16,128]{1,0:T(8,128)}, f32[16,128]{1,0:T(8,128)S(1)}, u32[]{:S(2)}) copy-start(f32[16,128]{1,0:T(8,128)S(1)} %shard_map.93.sums) | copy-start | bytes 24580

commit v5 on v4

--- a/solution.py
+++ b/solution.py
@@ -789,6 +789,7 @@
         out_shape=[jax.ShapeDtypeStruct((2, MODES, MODES), jnp.float32)] * 4,
         in_specs=[vmem],
         out_specs=[vmem] * 4,
+        compiler_params=pltpu.CompilerParams(vmem_limit_bytes=1024 * 1024),
     )(sums)
 
 

time: 43.2 us -> 41.9 us (0.970)
  Pallas kernels: 41.2 us -> 40.5 us
  local copies, waits for them, and re-layouts: 0.58 us -> 0 us
    pallas_call x1, Pallas kernels: 1.39 us -> 0.69 us  [per_device(): pl.pallas_call(lay_out, out_shape=[jax.ShapeDtypeStruct((2, MODES, MODES)...]
    unnamed x2 -> x0, local copies, waits for them, and re-layouts: 0.58 us -> none
where the time goes in v5:
time: 41.9 us; the launch traced here: 41.7 us
  Pallas kernels  40.5 us (97%)
  between operations  1.29 us (3%)
    pallas_call x1, Pallas kernels, insert_sums(): pl.pallas_call(functools.partial(hop_kernel, counts, comm), out_shape=plt...  39.8 us

profile of v5, /device:TPU:1, one launch (start us, length us, event | category | flops | bytes accessed | tf_op | source)
XLA Modules:
  0.0 41.7 jit_solution(17580166990547885803)
XLA Ops:
  1.3 39.8 %shard_map.93.sums = f32[16,128]{1,0:T(8,128)S(1)} custom-call(s32[1]{0:T(128)S(6)} %copy.10.start_hbm, s32[16]{0:T(128)} %charge_hbm.1, bf16[16,2,4,3,2,2,256]{6,5,4,3,2,1,0:T(2,128)(2,1)} %low_ref.1, f32[4,18,2,2,256]{4,3,2,1,0:T(2,128)} %link_ref.1, f32[4,2,2,256]{3,2,1,0:T(2,128)} %photon_ref.1, bf16[1536,128]{1,0:T(8,128)(2,1)} %constant.2.clone.table_ref), custom_call_target="tpu_custom_call" | custom-call | tf_op jit(solution)/shard_map/pallas_call | solution.py:733
  41.1 0.7 %shard_map.94 = (f32[2,16,16]{2,1,0:T(8,128)}, f32[2,16,16]{2,1,0:T(8,128)}, f32[2,16,16]{2,1,0:T(8,128)}, f32[2,16,16]{2,1,0:T(8,128)}) custom-call(f32[16,128]{1,0:T(8,128)S(1)} %shard_map.93.sums), custom_call_target="tpu_custom_call" | custom-call | tf_op jit(solution)/shard_map/pallas_call | solution.py:787

commit v6 on v5

--- a/solution.py
+++ b/solution.py
@@ -298,15 +298,15 @@
         others_y.append((peer_y, at(gz, peer_y * 4 + inner)))
     stages = ((others_x, x), (others_z, z), (others_y, y))
     crossed = ta + 1 - 2 * core
-    along_row = [(x, at(gz, crossed))]
-    along_row += [
+    along_row = [
         (wrapped(x + dx, 4), at(z_hi * 4 + wrapped(x + dx, 4), crossed)) for dx in (2, 1, 3)
     ]
-    along_column = [(y, at(gz, crossed))]
-    along_column += [
+    along_row.append((x, at(gz, crossed)))
+    along_column = [
         (wrapped(y + dy, 8), at(gz, wrapped(y + dy, 8) * 4 + crossed - y * 4))
         for dy in (4, 3, 5, 2, 6, 1, 7)
     ]
+    along_column.append((y, at(gz, crossed)))
     is_first, is_second = core == 0, core == 1
 
     below_z = at(jnp.where(gz == 0, n_gz - 1, gz - 1), ta)
@@ -699,7 +699,9 @@
                 slots[number, index] = total
                 targets = [(index, device) for _, device in others]
                 if number == 2:
-                    targets += [(index, device) for _, device in along_column]
+                    firsts = [(index, device) for _, device in along_column]
+                    pairs = zip(firsts[:-1], targets)
+                    targets = [target for two in pairs for target in two] + firsts[-1:]
                 for slot, device in targets:
                     copy = message(slots.at[number, index], number, slot, len(started), device)
                     copy.start()

time: 41.9 us -> 42.2 us (level)
  no operation moved by 1% of the time
where the time goes in v6:
time: 42.2 us; the launch traced here: 42 us
  Pallas kernels  40.8 us (97%)
  between operations  1.29 us (3%)
    pallas_call x1, Pallas kernels, insert_sums(): pl.pallas_call(functools.partial(hop_kernel, counts, comm), out_shape=plt...  40.1 us

profile of v6, /device:TPU:1, one launch (start us, length us, event | category | flops | bytes accessed | tf_op | source)
XLA Modules:
  0.0 42.0 jit_solution(10951337367409530553)
XLA Ops:
  1.3 40.1 %shard_map.93.sums = f32[16,128]{1,0:T(8,128)S(1)} custom-call(s32[1]{0:T(128)S(6)} %copy.10.start_hbm, s32[16]{0:T(128)} %charge_hbm.1, bf16[16,2,4,3,2,2,256]{6,5,4,3,2,1,0:T(2,128)(2,1)} %low_ref.1, f32[4,18,2,2,256]{4,3,2,1,0:T(2,128)} %link_ref.1, f32[4,2,2,256]{3,2,1,0:T(2,128)} %photon_ref.1, bf16[1536,128]{1,0:T(8,128)(2,1)} %constant.2.clone.table_ref), custom_call_target="tpu_custom_call" | custom-call | tf_op jit(solution)/shard_map/pallas_call | solution.py:735
  41.4 0.7 %shard_map.94 = (f32[2,16,16]{2,1,0:T(8,128)}, f32[2,16,16]{2,1,0:T(8,128)}, f32[2,16,16]{2,1,0:T(8,128)}, f32[2,16,16]{2,1,0:T(8,128)}) custom-call(f32[16,128]{1,0:T(8,128)S(1)} %shard_map.93.sums), custom_call_target="tpu_custom_call" | custom-call | tf_op jit(solution)/shard_map/pallas_call | solution.py:789
